TPU v7x, 256 devices: a whole 4x4x8 slice. The times are simulated.
256 devices in a mesh: dp: 4 (over y_lo, core), context: 32 (over x, z), tensor: 2 (over y_hi).
Axes of the slice: x: 4, y: 4 (y_hi: 2, y_lo: 2; y = y_hi * 2 + y_lo), z: 8, core: 2. Of those that a mesh axis runs over, the one named last changes fastest.
Arguments:
- queries: bfloat16 [16384, 2560], P(('dp', 'context'), 'tensor'), may hold values from -6 to 6
- key_rows: bfloat16 [16384, 2560], P(('dp', 'context'), 'tensor'), may hold values from -6 to 6
- value_rows: bfloat16 [16384, 2560], P(('dp', 'context'), 'tensor'), may hold values from -6 to 6
- gate_rows: bfloat16 [16384, 2560], P(('dp', 'context'), 'tensor'), may hold values from -6 to 6
- out_grad: bfloat16 [16384, 2560], P(('dp', 'context'), 'tensor'), may hold values from -6 to 6
- decay_rate: float32 [10], P('tensor'), may hold values from 3.0517578e-05 to 0.03125
- norm_gain: float32 [2560], P('tensor'), may hold values from 0.5 to 1.5
- reset_offsets: int32 [4, 16], P('dp'), may hold values from 0 to 128, as said below
- pair_prompts: int32 [4, 2], P('dp'), may hold values from 0 to 15
Outputs:
- retained: bfloat16 [16384, 2560], P(('dp', 'context'), 'tensor')
- grad_query: bfloat16 [16384, 2560], P(('dp', 'context'), 'tensor')
- grad_key: bfloat16 [16384, 2560], P(('dp', 'context'), 'tensor')
- grad_value: bfloat16 [16384, 2560], P(('dp', 'context'), 'tensor')
- grad_gate: bfloat16 [16384, 2560], P(('dp', 'context'), 'tensor')
- grad_gain: float32 [2560], P('tensor')
Inputs may be any that keep to these rules, and one draw needn't show every extreme that they name: `reset_offsets`: 128 means that no document starts in the shard.
All inputs are finite; a program needn't handle non-finite values.
Results may differ from a plain program's by a relative error of at most 0.0053.
Values sent between devices are 32-bit elements; how exact they have to be, the bound alone decides.
A program may use at most 128 MiB of HBM per device.

v0:
```python
import jax
import jax.numpy as jnp
from jax import lax
from jax.sharding import PartitionSpec as P


def entering(array, axis, combine, identity, reverse):
    size, place = (lax.axis_size(axis), lax.axis_index(axis))
    everything = jax.tree.map(lambda part: lax.all_gather(part, axis), array)
    start = jax.tree.map(
        lambda part, zero: jnp.broadcast_to(jnp.asarray(zero, part.dtype), part.shape),
        array,
        identity,
    )

    def lap(k, before):
        at = size - 1 - k if reverse else k
        reached = at > place if reverse else at < place
        new = combine(before, jax.tree.map(lambda part: part[at], everything))
        return jax.tree.map(lambda a, b: jnp.where(reached, a, b), new, before)

    return lax.fori_loop(0, size, lap, start)


def broadcast(array, axis, root):
    mine = lax.axis_index(axis) == root
    return lax.psum(jnp.where(mine, array, jnp.zeros_like(array)), axis)


def decay_tables(decay_rate, reset_point, length):
    positions = jnp.arange(length, dtype=jnp.int32)
    position_float = positions.astype(jnp.float32)
    later_doc = positions >= reset_point
    distance = position_float[:, None] - position_float[None, :]
    allowed = (distance >= 0.0) & (later_doc[:, None] == later_doc[None, :])
    decay_mask = jnp.where(
        allowed[None], jnp.exp(-decay_rate[:, None, None] * jnp.maximum(distance, 0.0)[None]), 0.0
    )
    into_weight = jnp.where(
        (positions < reset_point)[None],
        jnp.exp(-decay_rate[:, None] * (position_float + 1.0)[None]),
        0.0,
    )
    out_weight = jnp.where(
        (positions >= reset_point % length)[None],
        jnp.exp(-decay_rate[:, None] * (length - 1.0 - position_float)[None]),
        0.0,
    )
    link_decay = jnp.where(reset_point == length, jnp.exp(-decay_rate * length), 0.0)
    return (decay_mask, into_weight.T[:, :, None], out_weight.T[:, :, None], link_decay)


def finish(mixed, gate_value, gain_grid):
    centre = mixed - jnp.mean(mixed, axis=-1, keepdims=True)
    spread = jnp.mean(centre * centre, axis=-1, keepdims=True)
    return jax.nn.silu(gate_value) * (centre * lax.rsqrt(spread + 1e-05)) * gain_grid


def chain_combine(earlier, nearer):
    return (earlier[0] * nearer[0], nearer[0][:, None, None] * earlier[1] + nearer[1])


def per_device(
    queries,
    key_rows,
    value_rows,
    gate_rows,
    out_grad,
    decay_rate,
    norm_gain,
    reset_offsets,
    pair_prompts,
):
    length = queries.shape[0]
    head_count = decay_rate.shape[0]
    head_dim = queries.shape[1] // head_count
    grid_shape = (length, head_count, head_dim)
    key_scale = head_dim ** (-0.5)
    query_grid = queries.reshape(grid_shape)
    key_grid = key_rows.reshape(grid_shape)
    value_grid = value_rows.reshape(grid_shape)
    gain_grid = norm_gain.reshape(head_count, head_dim)
    pair_count = pair_prompts.shape[1]
    context_size = lax.axis_size("context")
    quarter = context_size // 4
    half_size = context_size // 2
    span_size = max(1, context_size // 8)
    position = lax.axis_index("context")
    prompt_index = position - quarter
    is_prompt = jnp.logical_and(position >= quarter, position < quarter + half_size)
    response_index = jnp.where(
        is_prompt, 0, jnp.where(position < quarter, position, position - half_size)
    )
    my_pair = jnp.where(is_prompt, -1, response_index // (2 * span_size))
    shard_depth = jnp.where(is_prompt, 0, response_index % span_size)
    is_first = jnp.logical_or(
        jnp.logical_and(jnp.logical_not(is_prompt), shard_depth == 0), position == quarter
    )
    prompt_slots = jnp.arange(half_size, dtype=jnp.int32)
    prompt_reset = jnp.sum(jnp.where(prompt_slots == prompt_index, reset_offsets[0], 0))
    reset_point = jnp.where(is_prompt, prompt_reset, length)
    decay_mask, into_weight, out_weight, link_decay = decay_tables(decay_rate, reset_point, length)
    scaled_keys = key_grid.astype(jnp.float32) * out_weight
    local_state = key_scale * jnp.einsum(
        "shd,she->hde", scaled_keys, value_grid, precision=lax.Precision.HIGHEST
    )
    scores = (
        jnp.einsum("thd,shd->hts", query_grid, key_grid, preferred_element_type=jnp.float32)
        * key_scale
    )
    weights = (scores * decay_mask).astype(jnp.bfloat16)
    intra = jnp.einsum("hts,shd->thd", weights, value_grid, preferred_element_type=jnp.float32)
    state_shape = (head_count, head_dim, head_dim)
    neutral = (jnp.ones((head_count,), jnp.float32), jnp.zeros(state_shape, jnp.float32))
    term_decay = jnp.where(is_first, 0.0, link_decay)
    chain_in = entering((term_decay, local_state), "context", chain_combine, neutral, False)[1]
    chain_in = jnp.where(is_first, 0.0, chain_in)
    prompt_end = term_decay[:, None, None] * chain_in + local_state
    pair_slots = jnp.arange(pair_count, dtype=jnp.int32)
    owner_here = jnp.logical_and(pair_prompts[0] == prompt_index, is_prompt)

    def take_seed(pair_now, seed_state):
        received = broadcast(prompt_end, "context", pair_prompts[0, pair_now] + quarter)
        return jnp.where(my_pair == pair_now, received, seed_state)

    seed_state = lax.fori_loop(0, pair_count, take_seed, jnp.zeros(state_shape, jnp.float32))
    seed_lift = jnp.where(
        is_prompt, 0.0, jnp.exp(-decay_rate * (length * shard_depth).astype(jnp.float32))
    )
    state_in = chain_in + seed_lift[:, None, None] * seed_state
    lifted = query_grid.astype(jnp.float32) * into_weight
    mixed = intra + jnp.einsum("thd,hde->the", lifted, state_in, precision=lax.Precision.HIGHEST)
    retained_full, pullback = jax.vjp(
        finish, mixed, gate_rows.reshape(grid_shape).astype(jnp.float32), gain_grid
    )
    grad_mixed, grad_gate, gain_part = pullback(out_grad.reshape(grid_shape).astype(jnp.float32))
    entry_grad = jnp.einsum("thd,the->hde", lifted, grad_mixed, precision=lax.Precision.HIGHEST)
    back_decay = jnp.where(is_first, 0.0, link_decay)
    back_entry = jnp.where(is_first, 0.0, entry_grad)
    later_grads = entering((back_decay, back_entry), "context", chain_combine, neutral, True)[1]
    grad_first = entry_grad + link_decay[:, None, None] * later_grads
    grad_table = jnp.where(
        ((pair_slots == my_pair) & is_first)[:, None, None, None], grad_first[None], 0.0
    )
    routed = lax.psum(grad_table, "context")
    owned_grads = jnp.sum(jnp.where(owner_here[:, None, None, None], routed, 0.0), axis=0)
    owner_slots = pair_prompts[0]
    reset_flags = reset_offsets[0] != length
    between = (
        (prompt_slots[None, :] > prompt_index)
        & (prompt_slots[None, :] <= owner_slots[:, None])
        & reset_flags[None, :]
    )
    blocked = jnp.sum(between.astype(jnp.int32), axis=1) > 0
    reaches = (owner_slots > prompt_index) & jnp.logical_not(blocked) & is_prompt
    hop_count = jnp.maximum(owner_slots - prompt_index, 0).astype(jnp.float32)
    reach_weight = jnp.where(
        reaches[:, None], jnp.exp(-decay_rate[None, :] * (length * hop_count)[:, None]), 0.0
    )
    carried = jnp.sum(reach_weight[:, :, None, None] * routed, axis=0)
    grad_state = later_grads + owned_grads + carried
    grad_low = grad_mixed.astype(jnp.bfloat16)
    grad_weights = (
        jnp.einsum("thd,shd->hts", grad_low, value_grid, preferred_element_type=jnp.float32)
        * decay_mask
    ).astype(jnp.bfloat16)
    grad_query = (
        jnp.einsum("hts,shd->thd", grad_weights, key_grid, preferred_element_type=jnp.float32)
        * key_scale
    )
    grad_query = (
        grad_query
        + jnp.einsum("the,hde->thd", grad_mixed, state_in, precision=lax.Precision.HIGHEST)
        * into_weight
    )
    grad_key = (
        jnp.einsum("hts,thd->shd", grad_weights, query_grid, preferred_element_type=jnp.float32)
        * key_scale
    )
    grad_key = (
        grad_key
        + key_scale
        * jnp.einsum("she,hde->shd", value_grid, grad_state, precision=lax.Precision.HIGHEST)
        * out_weight
    )
    grad_value = jnp.einsum("hts,thd->shd", weights, grad_low, preferred_element_type=jnp.float32)
    grad_value = grad_value + key_scale * jnp.einsum(
        "shd,hde->she", scaled_keys, grad_state, precision=lax.Precision.HIGHEST
    )
    token_total = length * context_size * lax.axis_size("dp")
    grad_gain = lax.psum(gain_part.reshape(-1), ("dp", "context")) / token_total**0.5
    flat_shape = (length, head_count * head_dim)
    return (
        retained_full.astype(jnp.bfloat16).reshape(flat_shape),
        grad_query.astype(jnp.bfloat16).reshape(flat_shape),
        grad_key.astype(jnp.bfloat16).reshape(flat_shape),
        grad_value.astype(jnp.bfloat16).reshape(flat_shape),
        grad_gate.astype(jnp.bfloat16).reshape(flat_shape),
        grad_gain,
    )


def solution(mesh):
    in_specs = (
        P(("dp", "context"), "tensor"),
        P(("dp", "context"), "tensor"),
        P(("dp", "context"), "tensor"),
        P(("dp", "context"), "tensor"),
        P(("dp", "context"), "tensor"),
        P("tensor"),
        P("tensor"),
        P("dp", None),
        P("dp", None),
    )
    out_specs = (
        P(("dp", "context"), "tensor"),
        P(("dp", "context"), "tensor"),
        P(("dp", "context"), "tensor"),
        P(("dp", "context"), "tensor"),
        P(("dp", "context"), "tensor"),
        P("tensor"),
    )
    return jax.shard_map(
        per_device, mesh=mesh, in_specs=in_specs, out_specs=out_specs, check_vma=False
    )
```

profile of v0, /device:TPU:18, one launch (start us, length us, event | category | flops | bytes accessed | tf_op | source)
XLA Modules:
  0.0 1338.1 jit_solution(2105644105488579065)
XLA Ops:
  17.0 2.0 copy.121
  22.7 66.7 %all-reduce = f32[160]{0:T(256)S(1)} all-reduce(f32[160]{0:T(256)S(1)} %get-tuple-element.443), channel_id=2, replica_groups=mesh['dp'=4,'context'=32,'tensor'=2] {'context'}, use_global_device_ids=true, to_apply=%add | all-reduce | flops 160 | bytes 1280
  91.4 2.0 copy.108
  96.6 204.0 %all-gather.6.cloned.1.call-done = f32[160,256,256]{2,1,0:T(8,128)} async-done(((f32[5,256,256]{2,1,0:T(8,128)}), f32[160,256,256]{2,1,0:T(8,128)}) %all-gather.6.cloned.1.call-update) | async-done | bytes 41943056 | tf_op jit(solution)/shard_map/all_gather | solution.py:9
  300.6 65.0 %while.44 = (s32[]{:T(128)}, f32[5,256,256]{2,1,0:T(8,128)S(1)}, s32[]{:T(128)}, f32[32,5]{1,0:T(8,128)S(1)}, f32[32,5,256,256]{3,2,1,0:T(8,128)}, /*index=5*/s32[]{:T(128)}, s32[]{:T(128)}) while((s32[]{:T(128)}, f32[5,256,256]{2,1,0:T(8,128)S(1)}, s32[]{:T(128)}, f32[32,5]{1,0:T(8,128)S(1)}, f32[32,5,256,256]{3,2,1,0:T(8,128)}, ...), condition=%wide.region_2.3_spmd.clone, body=%wide.region_1.2_spmd.clone.sunk | while | flops 1310724 | bytes 3932333 | solution.py:22
  365.6 2.6 multiply_add_fusion.2
  368.2 305.4 %while.45 = (s32[]{:T(128)}, f32[5,256,256]{2,1,0:T(8,128)S(1)}, s32[]{:T(128)}, s32[1,2]{1,0:T(1,128)S(1)}, f32[5,256,256]{2,1,0:T(8,128)}, /*index=5*/s32[]{:T(128)}, u32[]{:T(128)}, u32[]{:T(128)}, s32[]{:T(128)}) while((s32[]{:T(128)}, f32[5,256,256]{2,1,0:T(8,128)S(1)}, s32[]{:T(128)}, s32[1,2]{1,0:T(1,128)S(1)}, ...), condition=%wide.region_5.6_spmd.clone, body=%wide.region_3.5_spmd.clone.sunk | while | flops 1310729 | bytes 14418135 | solution.py:126
  370.7 149.6 %all-reduce.6.cloned.1.call-done = f32[5,256,256]{2,1,0:T(8,128)} async-done(((f32[5,256,256]{2,1,0:T(8,128)}), f32[5,256,256]{2,1,0:T(8,128)}) %all-reduce.6.cloned.1.call-update) | async-done | bytes 1310736 | tf_op jit(solution)/shard_map/while/body/eval_jaxpr/psum | solution.py:27
  523.3 150.0 %all-reduce.6.cloned.1.call-done = f32[5,256,256]{2,1,0:T(8,128)} async-done(((f32[5,256,256]{2,1,0:T(8,128)}), f32[5,256,256]{2,1,0:T(8,128)}) %all-reduce.6.cloned.1.call-update) | async-done | bytes 1310736 | tf_op jit(solution)/shard_map/while/body/eval_jaxpr/psum | solution.py:27
  673.8 2.7 fusion.39
  678.8 3.0 broadcast_select_fusion.2
  682.1 280.8 %all-gather.8.cloned.1.call-done = f32[160,256,256]{2,1,0:T(8,128)} async-done(((f32[5,256,256]{2,1,0:T(8,128)}), f32[160,256,256]{2,1,0:T(8,128)}) %all-gather.8.cloned.1.call-update) | async-done | bytes 41943056 | tf_op jit(solution)/shard_map/all_gather | solution.py:9
  962.8 65.3 %while.46 = (s32[]{:T(128)}, f32[5,256,256]{2,1,0:T(8,128)S(1)}, s32[]{:T(128)}, f32[32,5]{1,0:T(8,128)S(1)}, f32[32,5,256,256]{3,2,1,0:T(8,128)}, /*index=5*/s32[]{:T(128)}, s32[]{:T(128)}, s32[]{:T(128)}, s32[]{:T(128)}) while((s32[]{:T(128)}, f32[5,256,256]{2,1,0:T(8,128)S(1)}, s32[]{:T(128)}, f32[32,5]{1,0:T(8,128)S(1)}, ...), condition=%wide.region_11.12_spmd.clone, body=%wide.region_10.11_spmd.clone.sunk | while | flops 1310728 | bytes 3932395 | solution.py:22
  964.9 2.0 fusion.57
  966.9 2.0 fusion.57
  969.0 2.0 fusion.57
  971.0 2.0 fusion.57
  973.0 2.0 fusion.57
  975.1 2.0 fusion.57
  977.1 2.0 fusion.57
  1039.9 2.4 fusion.10
  1045.6 270.7 %psum.26 = f32[1280]{0:T(1024)S(1)} all-reduce(f32[1280]{0:T(1024)S(1)} %reshape.367), channel_id=1, replica_groups=mesh['dp'=4,'context'=32,'tensor'=2] {'dp','context'}, use_global_device_ids=true, to_apply=%region_17.18 | all-reduce | flops 1280 | bytes 10240 | tf_op jit(solution)/shard_map/psum | solution.py:191
  1319.4 2.7 select_reduce_fusion
  1326.9 3.7 fusion.11
  (239 shorter events, 161.8 us)
Async XLA Ops:
  7.2 4.7 copy-start.21
  7.2 5.9 copy-start.19
  7.2 293.4 %all-gather.6.cloned.1.call-start = ((), (), s32[]{:S(2)}) async-start(), calls=%async_computation.1 | async-start | bytes 43253760 | tf_op jit(solution)/shard_map/all_gather | solution.py:9
  10.5 83.1 %copy-start.7 = (bf16[128,1280]{0,1:T(8,128)(2,1)}, bf16[128,1280]{0,1:T(8,128)(2,1)S(1)}, u32[]{:S(2)}) copy-start(bf16[128,1280]{0,1:T(8,128)(2,1)S(1)} %copy.110) | copy-start | bytes 983044
  11.8 83.1 %copy-start.3 = (bf16[128,1280]{0,1:T(8,128)(2,1)}, bf16[128,1280]{0,1:T(8,128)(2,1)S(1)}, u32[]{:S(2)}) copy-start(bf16[128,1280]{0,1:T(8,128)(2,1)S(1)} %copy.113) | copy-start | bytes 983044
  20.8 72.5 %copy-start.15 = (f32[1280]{0:T(1024)S(1)}, f32[1280]{0:T(1024)}, u32[]{:S(2)}) copy-start(f32[1280]{0:T(1024)} %param.21) | copy-start | bytes 15364
  365.6 2.6 copy-start.18
  368.2 305.5 %copy-start.9 = (bf16[128,5,256]{2,0,1:T(8,128)(2,1)S(1)}, bf16[128,5,256]{2,0,1:T(8,128)(2,1)}, u32[]{:S(2)}) copy-start(bf16[128,5,256]{2,0,1:T(8,128)(2,1)} %copy.116) | copy-start | bytes 983044
  368.2 152.1 %all-reduce.6.cloned.1.call-start = ((), (), s32[]{:S(2)}) async-start(), calls=%async_computation.3 | async-start | bytes 2621440 | tf_op jit(solution)/shard_map/while/body/eval_jaxpr/psum | solution.py:27
  520.7 152.5 %all-reduce.6.cloned.1.call-start = ((), (), s32[]{:S(2)}) async-start(), calls=%async_computation.3 | async-start | bytes 2621440 | tf_op jit(solution)/shard_map/while/body/eval_jaxpr/psum | solution.py:27
  673.7 2.8 copy-start
  673.7 289.2 %all-gather.8.cloned.1.call-start = ((), (), s32[]{:S(2)}) async-start(), calls=%async_computation.2 | async-start | bytes 43253760 | tf_op jit(solution)/shard_map/all_gather | solution.py:9
  673.7 3.1 copy-start.5
  673.7 3.1 copy-start.6
  681.8 637.6 %all-reduce.4.cloned.1.call-start = ((), (), s32[]{:S(2)}) async-start(), calls=%async_computation | async-start | bytes 5242880 | tf_op jit(solution)/shard_map/psum | solution.py:145
  1037.3 2.6 copy-start.1
  1042.4 2.2 copy-start.12
  1042.4 274.6 %copy-start.10 = (bf16[128,1280]{0,1:T(8,128)(2,1)S(1)}, bf16[128,1280]{0,1:T(8,128)(2,1)}, u32[]{:S(2)}) copy-start(bf16[128,1280]{0,1:T(8,128)(2,1)} %copy.109) | copy-start | bytes 983044
  1044.5 273.6 %copy-start.14 = (bf16[5,128,128]{2,1,0:T(8,128)(2,1)S(1)}, bf16[5,128,128]{2,1,0:T(8,128)(2,1)}, u32[]{:S(2)}) copy-start(bf16[5,128,128]{2,1,0:T(8,128)(2,1)} %copy-done.13) | copy-start | bytes 491524
  1316.9 2.4 copy-start.16
  1317.0 2.4 copy-start.17
  1319.4 3.8 copy-start.4
  1319.4 3.8 copy-start.11
  1324.2 2.8 copy-start.8
  (3 other events, 2.4 us)
Sparse Core Ops, SparseCore 0:
  15.2 285.3 all-gather.5
  372.5 147.7 all-reduce.5
  525.0 148.1 all-reduce.5
  681.9 280.8 all-gather.7
  1031.6 153.8 all-reduce.3
where the time goes:
time: 1350 us; the launch traced here: 1340 us
  waiting for transfers between devices  784 us (58%)
  blocking collectives  337 us (25%)
  other arithmetic  146 us (11%)
  local copies, waits for them, and re-layouts  28.4 us (2%)
  matrix products  22 us (2%)
  between operations  15.5 us (1%)
    all_gather x2, waiting for transfers between devices, entering(): everything = jax.tree.map(lambda part: lax.all_gather(part, axis), array)  485 us
    psum x2, waiting for transfers between devices, broadcast(): return lax.psum(jnp.where(mine, array, jnp.zeros_like(array)), axis)  300 us
    psum x1, blocking collectives, per_device(): lax.psum(gain_part.reshape(-1), ('dp', 'context')) / token_total ** 0.5  271 us
    select_n x64, other arithmetic, lap(): return jax.tree.map(lambda a, b: jnp.where(reached, a, b), new, before)  127 us
    unnamed x1, blocking collectives  66.7 us
  transfers between devices with their start and end apart: 5, of which 4 were waited for; matrix products, arithmetic and copies ran while one was open for 2% of the time, Pallas kernels for 0%

commit v1 on v0

v1 whole, which is shorter than its diff:
```python
import functools

import jax
import jax.numpy as jnp
from jax import lax
from jax.experimental import pallas as pl
from jax.experimental.pallas import tpu as pltpu
from jax.sharding import PartitionSpec as P

MESH = pl.DeviceIdType.MESH
F32 = jnp.float32
BF16 = jnp.bfloat16

ROW = 8
ROWS = 4
HD = 256
TOK = 128
SL = HD // ROW
SPAN = 4


def dot(a, b, ca, cb):
    return lax.dot_general(a, b, (((ca,), (cb,)), ((), ())), preferred_element_type=F32)


def split(x):
    hi = x.astype(BF16)
    return hi, (x - hi.astype(F32)).astype(BF16)


def remote(src, dst, send_sem, recv_sem, **where):
    return pltpu.make_async_remote_copy(
        src_ref=src,
        dst_ref=dst,
        send_sem=send_sem,
        recv_sem=recv_sem,
        device_id=where,
        device_id_type=MESH,
    )


def kernel(
    heads,
    n_dp,
    rate,
    resets,
    pairs,
    q_ref,
    k_ref,
    v_ref,
    g_ref,
    do_ref,
    gain_ref,
    ret_ref,
    dq_ref,
    dk_ref,
    dv_ref,
    dgate_ref,
    dgain_ref,
    l_buf,
    r1,
    o2,
    s_buf,
    e_buf,
    r3,
    o4,
    g_buf,
    t_out,
    t_in,
    c_out,
    c_in,
    b_out,
    b_in,
    dkp,
    dvp,
    gp,
    gz,
    gx_out,
    gx,
    gd_out,
    gd,
    ss,
    rs,
    xs,
    xr,
    gs,
    gr,
):
    me = lax.axis_index("context")
    my_dp = lax.axis_index("dp")
    x, z = me // ROW, lax.rem(me, ROW)
    is_prompt = jnp.logical_and(x >= 1, x <= 2)
    scale = HD**-0.5

    def ctx(xx, zz):
        return xx * ROW + lax.rem(zz + 2 * ROW, ROW)

    barrier = pltpu.get_barrier_semaphore()

    def greet_z(k, c):
        pl.semaphore_signal(
            barrier, inc=1, device_id={"context": ctx(x, z + k)}, device_id_type=MESH
        )
        return c

    def greet_x(k, c):
        pl.semaphore_signal(
            barrier, inc=1, device_id={"context": ctx(lax.rem(x + k, ROWS), z)}, device_id_type=MESH
        )
        return c

    def greet_dp(k, c):
        pl.semaphore_signal(
            barrier, inc=1, device_id={"dp": lax.rem(my_dp + k, n_dp)}, device_id_type=MESH
        )
        return c

    lax.fori_loop(1, ROW, greet_z, 0)
    lax.fori_loop(1, ROWS, greet_x, 0)
    lax.fori_loop(1, n_dp, greet_dp, 0)
    pl.semaphore_wait(barrier, ROW - 1 + ROWS - 1 + n_dp - 1)

    prompt_index = jnp.clip(me - ROW, 0, 2 * ROW - 1)
    rho = jnp.where(is_prompt, resets[0, prompt_index], TOK)

    def cols(h):
        return pl.ds(pl.multiple_of(h * HD, HD), HD)

    def column_weights(h):
        lam = rate[h]
        t = lax.broadcasted_iota(jnp.int32, (TOK, 1), 0)
        tf = t.astype(F32)
        into = jnp.where(t < rho, jnp.exp(-lam * (tf + 1.0)), 0.0)
        out = jnp.where(t >= lax.rem(rho, TOK), jnp.exp(-lam * (TOK - 1.0 - tf)), 0.0)
        return into, out

    def own_rows(zz):
        return pl.ds(pl.multiple_of(zz * SL, SL), SL)

    def to_owners(src, dst, phase, h):
        def one(k, c):
            zz = lax.rem(z + k, ROW)
            remote(
                src.at[h, own_rows(zz)],
                dst.at[h, k],
                ss.at[phase, h],
                rs.at[phase, h],
                context=x * ROW + zz,
            ).start()
            return c

        lax.fori_loop(1, ROW, one, 0)
        dst[h, 0] = src[h, own_rows(z)]

    def from_owner(src, dst, phase, h):
        def one(k, c):
            remote(
                src.at[h, k],
                dst.at[h, own_rows(z)],
                ss.at[phase, h],
                rs.at[phase, h],
                context=ctx(x, z - k),
            ).start()
            return c

        lax.fori_loop(1, ROW, one, 0)
        dst[h, own_rows(z)] = src[h, 0]

    def wait_row(buf, phase, h, send):
        ref = buf.at[h, pl.ds(1, ROW - 1)]
        c = remote(ref, ref, ss.at[phase, h], rs.at[phase, h], context=ctx(x, z + 1))
        if send:
            c.wait_send()
        else:
            c.wait_recv()

    def wait_full(buf, phase, h):
        ref = buf.at[h, pl.ds(0, HD - SL)]
        remote(ref, ref, ss.at[phase, h], rs.at[phase, h], context=ctx(x, z + 1)).wait_recv()

    def stage_a(h, c):
        _, out = column_weights(h)
        kw = k_ref[:, cols(h)].astype(F32) * (out * scale)
        hi, lo = split(kw)
        vh = v_ref[:, cols(h)]
        l_buf[h] = dot(hi, vh, 0, 0) + dot(lo, vh, 0, 0)
        to_owners(l_buf, r1, 0, h)
        return c

    lax.fori_loop(0, heads, stage_a, 0)

    def decay_row(h):
        return jnp.exp(jnp.full((1, HD), -float(TOK) * rate[h], F32))

    def link(h, j, row):
        return row * (resets[0, j] == TOK).astype(F32)

    def x_send(src, dst, kind, h, xx):
        return remote(src, dst, xs.at[kind, h], xr.at[kind, h], context=ctx(xx, z))

    def forward_prompt(h, first, start):
        row = decay_row(h)

        def step(jz, carry):
            s, c0, c1 = carry
            j = first + jz
            slot = lax.rem(z - jz + ROW, ROW)
            o2[h, slot] = s
            s = s * link(h, j, row) + r1[h, slot]
            c0 = c0 + s * (pairs[0, 0] == j).astype(F32)
            c1 = c1 + s * (pairs[0, 1] == j).astype(F32)
            return s, c0, c1

        zero = jnp.zeros((SL, HD), F32)
        s, c0, c1 = lax.fori_loop(0, ROW, step, (start, zero, zero))
        c_out[h, 0] = c0
        c_out[h, 1] = c1
        return s

    def stage_b(h, c):
        wait_row(r1, 0, h, False)

        @pl.when(x == 1)
        def _():
            t_out[h] = forward_prompt(h, 0, jnp.zeros((SL, HD), F32))
            x_send(t_out.at[h], t_in.at[h], 0, h, 2).start()
            x_send(c_out.at[h, 0], c_in.at[h, 0], 1, h, 0).start()
            x_send(c_out.at[h, 1], c_in.at[h, 0], 1, h, 3).start()

        @pl.when(x == 2)
        def _():
            x_send(t_out.at[h], t_in.at[h], 0, h, 2).wait_recv()
            forward_prompt(h, ROW, t_in[h])
            x_send(c_out.at[h, 0], c_in.at[h, 1], 1, h, 0).start()
            x_send(c_out.at[h, 1], c_in.at[h, 1], 1, h, 3).start()

        @pl.when(jnp.logical_not(is_prompt))
        def _():
            x_send(c_out.at[h], c_in.at[h], 1, h, 1).wait_recv()
            row = decay_row(h)

            def side(sd, cc):
                def step(m, s):
                    slot = lax.rem(z - sd * SPAN - m + ROW, ROW)
                    o2[h, slot] = s
                    return s * row + r1[h, slot]

                lax.fori_loop(0, SPAN, step, c_in[h, 0] + c_in[h, 1])
                return cc

            lax.fori_loop(0, ROW // SPAN, side, 0)

        from_owner(o2, s_buf, 1, h)
        return c

    lax.fori_loop(0, heads, stage_b, 0)

    gp[...] = jnp.zeros_like(gp)

    def stage_c(h, c):
        lam = rate[h]
        into, out = column_weights(h)
        ti = lax.broadcasted_iota(jnp.int32, (TOK, TOK), 0)
        si = lax.broadcasted_iota(jnp.int32, (TOK, TOK), 1)
        dist = (ti - si).astype(F32)
        allowed = (ti >= si) & ((ti >= rho) == (si >= rho))
        mask = jnp.where(allowed, jnp.exp(-lam * jnp.maximum(dist, 0.0)), 0.0)
        qh, kh, vh = q_ref[:, cols(h)], k_ref[:, cols(h)], v_ref[:, cols(h)]
        weights = (dot(qh, kh, 1, 1) * scale * mask).astype(BF16)
        mixed = dot(weights, vh, 1, 0)
        wait_full(s_buf, 1, h)
        s_hi, s_lo = split(s_buf[h])
        mixed = mixed + into * (dot(qh, s_hi, 1, 0) + dot(qh, s_lo, 1, 0))
        centre = mixed - jnp.mean(mixed, axis=1, keepdims=True)
        r = lax.rsqrt(jnp.mean(centre * centre, axis=1, keepdims=True) + 1e-05)
        xhat = centre * r
        gain = gain_ref[:, cols(h)]
        gate = g_ref[:, cols(h)].astype(F32)
        go = do_ref[:, cols(h)].astype(F32)
        sig = 1.0 / (1.0 + jnp.exp(-gate))
        silu = gate * sig
        ret_ref[:, cols(h)] = (silu * xhat * gain).astype(BF16)
        gox = go * xhat
        dgate_ref[:, cols(h)] = (gox * gain * (sig + silu * (1.0 - sig))).astype(BF16)
        gp[pl.ds(h, 1), :] = jnp.sum(gox * silu, axis=0, keepdims=True)
        dx = go * silu * gain
        dx = dx - jnp.mean(dx, axis=1, keepdims=True) - xhat * jnp.mean(
            dx * xhat, axis=1, keepdims=True
        )
        gm = dx * r
        e_hi, e_lo = split(gm * into)
        e_buf[h] = dot(qh, e_hi, 0, 0) + dot(qh, e_lo, 0, 0)
        to_owners(e_buf, r3, 2, h)
        low, rest = split(gm)
        gw = (dot(low, vh, 1, 1) * mask).astype(BF16)
        inter = dot(low, s_hi, 1, 1) + dot(low, s_lo, 1, 1) + dot(rest, s_hi, 1, 1)
        dq_ref[:, cols(h)] = (dot(gw, kh, 1, 0) * scale + inter * into).astype(BF16)
        dkp[h] = dot(gw, qh, 0, 0) * scale
        dvp[h] = dot(weights, low, 0, 0)
        return c

    lax.fori_loop(0, heads, stage_c, 0)

    def gain_z(k, c):
        remote(gp, gz.at[z], gs.at[0], gr.at[0], context=ctx(x, z + k)).start()
        return c

    lax.fori_loop(1, ROW, gain_z, 0)
    gz[z] = gp[...]

    def backward_prompt(h, first, start):
        row = decay_row(h)

        def step(i, g):
            jz = ROW - 1 - i
            j = first + jz
            slot = lax.rem(z - jz + ROW, ROW)
            g = g + b_in[h, 0] * (pairs[0, 0] == j).astype(F32)
            g = g + b_in[h, 1] * (pairs[0, 1] == j).astype(F32)
            o4[h, slot] = g
            return r3[h, slot] + g * link(h, j, row)

        return lax.fori_loop(0, ROW, step, start)

    def stage_d(h, c):
        wait_row(r3, 2, h, False)

        @pl.when(jnp.logical_not(is_prompt))
        def _():
            row = decay_row(h)

            def side(sd, total):
                def step(i, g):
                    slot = lax.rem(z - sd * SPAN - (SPAN - 1 - i) + ROW, ROW)
                    o4[h, slot] = g
                    return r3[h, slot] + g * row

                return total + lax.fori_loop(0, SPAN, step, jnp.zeros((SL, HD), F32))

            b_out[h] = lax.fori_loop(0, ROW // SPAN, side, jnp.zeros((SL, HD), F32))
            pair = x // 3
            x_send(b_out.at[h], b_in.at[h, pair], 3, h, 2).start()
            x_send(b_out.at[h], b_in.at[h, pair], 3, h, 1).start()

        @pl.when(is_prompt)
        def _():
            x_send(c_out.at[h], b_in.at[h], 3, h, 0).wait_recv()

        @pl.when(x == 2)
        def _():
            t_out[h] = backward_prompt(h, ROW, jnp.zeros((SL, HD), F32))
            x_send(t_out.at[h], t_in.at[h], 2, h, 1).start()

        @pl.when(x == 1)
        def _():
            x_send(t_out.at[h], t_in.at[h], 2, h, 2).wait_recv()
            backward_prompt(h, 0, t_in[h])

        from_owner(o4, g_buf, 3, h)
        return c

    lax.fori_loop(0, heads, stage_d, 0)

    w = gz.at[pl.ds(0, ROW - 1)]
    remote(w, w, gs.at[0], gr.at[0], context=ctx(x, z + 1)).wait()

    gx_out[...] = lax.fori_loop(1, ROW, lambda i, a: a + gz[i], gz[0])

    def gain_x(k, c):
        remote(
            gx_out, gx.at[x], gs.at[1], gr.at[1], context=ctx(lax.rem(x + k, ROWS), z)
        ).start()
        return c

    lax.fori_loop(1, ROWS, gain_x, 0)
    gx[x] = gx_out[...]

    def gain_dp(k, c):
        remote(gd_out, gd.at[my_dp], gs.at[2], gr.at[2], dp=lax.rem(my_dp + k, n_dp)).start()
        return c

    def stage_e(h, c):
        wait_full(g_buf, 3, h)
        _, out = column_weights(h)
        out = out * scale
        g_hi, g_lo = split(g_buf[h])
        kh, vh = k_ref[:, cols(h)], v_ref[:, cols(h)]
        dk_ref[:, cols(h)] = (
            dkp[h] + out * (dot(vh, g_hi, 1, 1) + dot(vh, g_lo, 1, 1))
        ).astype(BF16)
        dv_ref[:, cols(h)] = (
            dvp[h] + out * (dot(kh, g_hi, 1, 0) + dot(kh, g_lo, 1, 0))
        ).astype(BF16)

        @pl.when(h == heads // 2)
        def _():
            w = gx.at[pl.ds(0, ROWS - 1)]
            remote(w, w, gs.at[1], gr.at[1], context=ctx(x, z + 1)).wait()
            gd_out[...] = gx[0] + gx[1] + gx[2] + gx[3]
            lax.fori_loop(1, n_dp, gain_dp, 0)
            gd[my_dp] = gd_out[...]

        return c

    lax.fori_loop(0, heads, stage_e, 0)

    w = gd.at[pl.ds(0, n_dp - 1)]
    remote(w, w, gs.at[2], gr.at[2], context=ctx(x, z + 1)).wait()
    token_total = TOK * ROW * ROWS * n_dp
    dgain_ref[...] = lax.fori_loop(1, n_dp, lambda i, a: a + gd[i], gd[0]) * (token_total**-0.5)

    def drain(h, c):
        wait_row(r1, 0, h, True)
        wait_row(o2, 1, h, True)
        wait_row(r3, 2, h, True)
        wait_row(o4, 3, h, True)

        @pl.when(x == 1)
        def _():
            x_send(t_out.at[h], t_in.at[h], 0, h, 2).wait_send()

        @pl.when(x == 2)
        def _():
            x_send(t_out.at[h], t_in.at[h], 2, h, 1).wait_send()

        @pl.when(is_prompt)
        def _():
            x_send(c_out.at[h], c_in.at[h], 1, h, 0).wait_send()

        @pl.when(jnp.logical_not(is_prompt))
        def _():
            x_send(c_out.at[h], b_in.at[h], 3, h, 1).wait_send()

        return c

    lax.fori_loop(0, heads, drain, 0)


def solution(mesh):
    n_dp = mesh.shape["dp"]
    assert mesh.shape["context"] == ROW * ROWS

    def per_device(
        queries,
        key_rows,
        value_rows,
        gate_rows,
        out_grad,
        decay_rate,
        norm_gain,
        reset_offsets,
        pair_prompts,
    ):
        heads = decay_rate.shape[0]
        flat = jax.ShapeDtypeStruct(queries.shape, BF16)
        vmem = pl.BlockSpec(memory_space=pltpu.VMEM)
        smem = pl.BlockSpec(memory_space=pltpu.SMEM)
        state = pltpu.VMEM((heads, HD, HD), F32)
        slots = pltpu.VMEM((heads, ROW, SL, HD), F32)
        piece = pltpu.VMEM((heads, SL, HD), F32)
        two = pltpu.VMEM((heads, 2, SL, HD), F32)
        part = pltpu.VMEM((heads, TOK, HD), F32)
        small = pltpu.VMEM((8, HD), F32)
        dma = pltpu.SemaphoreType.DMA
        outs = pl.pallas_call(
            functools.partial(kernel, heads, n_dp),
            out_shape=(flat, flat, flat, flat, flat, jax.ShapeDtypeStruct((8, HD), F32)),
            in_specs=[smem] * 3 + [vmem] * 6,
            out_specs=(vmem,) * 6,
            scratch_shapes=[
                state,
                slots,
                slots,
                state,
                state,
                slots,
                slots,
                state,
                piece,
                piece,
                two,
                two,
                piece,
                two,
                part,
                part,
                small,
                pltpu.VMEM((ROW, 8, HD), F32),
                small,
                pltpu.VMEM((ROWS, 8, HD), F32),
                small,
                pltpu.VMEM((n_dp, 8, HD), F32),
                dma((4, heads)),
                dma((4, heads)),
                dma((4, heads)),
                dma((4, heads)),
                dma((3,)),
                dma((3,)),
            ],
            compiler_params=pltpu.CompilerParams(
                collective_id=0, has_side_effects=True, vmem_limit_bytes=40 << 20
            ),
        )(
            decay_rate,
            reset_offsets,
            pair_prompts,
            queries,
            key_rows,
            value_rows,
            gate_rows,
            out_grad,
            norm_gain.reshape(1, -1),
        )
        return outs[:5] + (outs[5][:heads].reshape(-1),)

    rows = P(("dp", "context"), "tensor")
    in_specs = (rows,) * 5 + (P("tensor"), P("tensor"), P("dp", None), P("dp", None))
    return jax.shard_map(
        per_device,
        mesh=mesh,
        in_specs=in_specs,
        out_specs=(rows,) * 5 + (P("tensor"),),
        check_vma=False,
    )
```

time: 1350 us -> 136 us (0.10)
  waiting for transfers between devices: 784 us -> 0 us
  blocking collectives: 337 us -> 0 us
  other arithmetic: 146 us -> 0 us
  Pallas kernels: 0 us -> 124 us
  matrix products: 22 us -> 0 us
  local copies, waits for them, and re-layouts: 28.4 us -> 9.81 us
  between operations: 15.5 us -> 0.69 us
    all_gather x2 -> x0, waiting for transfers between devices: 485 us -> none  [entering(): everything = jax.tree.map(lambda part: lax.all_gather(part, axis), array)]
    psum x3 -> x0, waiting for transfers between devices: 300 us -> none  [the longest x2 300 us: broadcast(): return lax.psum(jnp.where(mine, array, jnp.zeros_like(array)), axis)]
    psum x1 -> x0, blocking collectives: 271 us -> none  [per_device(): lax.psum(gain_part.reshape(-1), ('dp', 'context')) / token_total ** 0.5]
    select_n x70 -> x0, other arithmetic: 133 us -> none  [the longest x64 127 us: lap(): return jax.tree.map(lambda a, b: jnp.where(reached, a, b), new, before)]
    pallas_call x0 -> x1, Pallas kernels: none -> 124 us  [per_device(): pl.pallas_call(functools.partial(kernel, heads, n_dp), out_shape=(flat, f...]
    unnamed x1 -> x0, blocking collectives: 66.7 us -> none
    dot_general x12 -> x0, matrix products: 22 us -> none  [the longest x1 3.72 us: per_device(): jnp.einsum('shd,hde->she', scaled_keys, grad_state, precision=lax.Precisi...]
  transfers between devices with their start and end apart: 5 -> 0, of which waited for: 4 -> 0; matrix products, arithmetic and copies ran while one was open for 2% -> 0% of each run, Pallas kernels for 0% -> 0%
where the time goes in v1:
time: 136 us; the launch traced here: 135 us
  Pallas kernels  124 us (91%)
  local copies, waits for them, and re-layouts  9.81 us (7%)
    pallas_call x1, Pallas kernels, per_device(): pl.pallas_call(functools.partial(kernel, heads, n_dp), out_shape=(flat, f...  124 us
    unnamed x21, local copies, waits for them, and re-layouts  8.49 us

profile of v1, /device:TPU:18, one launch (start us, length us, event | category | flops | bytes accessed | tf_op | source)
XLA Modules:
  0.0 134.9 jit_solution(5191962834841608716)
XLA Ops:
  0.6 0.0 copy-start.7
  0.6 0.0 copy-start.6
  0.7 0.0 copy-start.5
  0.7 0.7 reshape.18.gain_ref
  1.4 0.0 copy-done.7
  1.4 0.0 copy-done.6
  1.4 0.0 copy-done.5
  1.4 0.0 copy-start
  1.4 1.0 copy-done
  2.4 0.0 copy-start.1
  2.4 1.0 copy-done.1
  3.3 0.0 copy-start.2
  3.4 1.0 copy-done.2
  4.3 0.0 copy-start.3
  4.3 1.0 copy-done.3
  5.3 0.0 copy-start.4
  5.3 1.0 copy-done.4
  6.3 124.4 %shard_map.136 = (bf16[128,1280]{1,0:T(8,128)(2,1)S(1)}, bf16[128,1280]{1,0:T(8,128)(2,1)S(1)}, bf16[128,1280]{1,0:T(8,128)(2,1)S(1)}, bf16[128,1280]{1,0:T(8,12...) custom-call(f32[5]{0:T(128)S(1)} %copy-done.5, s32[1,16]{1,0:T(1,128)S(1)} %copy-done.6, ...), custom_call_target="tpu_custom_call" | custom-call | tf_op jit(solution)/shard_map/pallas_call | solution.py:465
  130.7 0.6 reshape.19
  131.3 0.7 copy.20
  132.0 0.7 copy.21
  132.7 0.7 copy.22
  133.5 0.7 copy.23
  134.2 0.7 copy.24
Async XLA Ops:
  0.6 0.8 copy-start.7
  0.6 0.7 copy-start.6
  0.7 0.7 copy-start.5
  1.4 1.0 copy-start
  2.4 1.0 copy-start.1
  3.3 1.0 copy-start.2
  4.3 1.0 copy-start.3
  5.3 1.0 copy-start.4

commit v2 on v1

v2 whole, which is shorter than its diff:
```python
import functools

import jax
import jax.numpy as jnp
from jax import lax
from jax.experimental import pallas as pl
from jax.experimental.pallas import tpu as pltpu
from jax.sharding import PartitionSpec as P

MESH = pl.DeviceIdType.MESH
F32 = jnp.float32
BF16 = jnp.bfloat16

ROW = 8
ROWS = 4
HD = 256
TOK = 128
SPAN = 4
PROMPTS = 16
OWNERS = 16
SL = HD // OWNERS
PARTS = 4
PR = HD // PARTS


def dot(a, b, ca, cb):
    return lax.dot_general(a, b, (((ca,), (cb,)), ((), ())), preferred_element_type=F32)


def split(x):
    hi = x.astype(BF16)
    return hi, (x - hi.astype(F32)).astype(BF16)


def remote(src, dst, send_sem, recv_sem, **where):
    return pltpu.make_async_remote_copy(
        src_ref=src,
        dst_ref=dst,
        send_sem=send_sem,
        recv_sem=recv_sem,
        device_id=where,
        device_id_type=MESH,
    )


def kernel(
    heads,
    n_dp,
    rate,
    resets,
    pairs,
    gain_ref,
    q_hbm,
    k_hbm,
    v_hbm,
    g_hbm,
    do_hbm,
    ret_hbm,
    dq_hbm,
    dk_hbm,
    dv_hbm,
    dgate_hbm,
    dgain_ref,
    q_ref,
    k_ref,
    v_ref,
    g_ref,
    do_ref,
    ret_ref,
    dq_ref,
    dk_ref,
    dv_ref,
    dgate_ref,
    l_buf,
    s_buf,
    eo_buf,
    e_buf,
    n_buf,
    no_buf,
    x_buf,
    r1,
    o2,
    r3,
    o4,
    dkp,
    dvp,
    gp,
    gz,
    gx_out,
    gx,
    gd_out,
    gd,
    ss,
    rs,
    cs,
    cr,
    bs,
    br,
    gs,
    gr,
    in_sem,
    out_sem,
):
    me = lax.axis_index("context")
    my_dp = lax.axis_index("dp")
    x, z = me // ROW, lax.rem(me, ROW)
    m = lax.rem(z, SPAN)
    block = me // SPAN
    is_prompt = jnp.logical_and(x >= 1, x <= 2)
    is_owner = jnp.logical_not(is_prompt)
    w = jnp.where(x == ROWS - 1, ROW, 0) + z
    prompt_index = jnp.clip(me - ROW, 0, PROMPTS - 1)
    first_prompt = jnp.logical_and(is_prompt, m == 0)
    first_response = jnp.logical_and(is_owner, m == 0)
    start_of_all = me == ROW
    scale = HD**-0.5

    loads = [
        pltpu.make_async_copy(src, dst, in_sem.at[i])
        for i, (src, dst) in enumerate(
            ((k_hbm, k_ref), (v_hbm, v_ref), (q_hbm, q_ref), (g_hbm, g_ref), (do_hbm, do_ref))
        )
    ]
    for load in loads:
        load.start()

    n_context = ROW * ROWS
    barrier = pltpu.get_barrier_semaphore()

    def greet(k, c):
        pl.semaphore_signal(
            barrier,
            inc=1,
            device_id={"context": lax.rem(me + k, n_context)},
            device_id_type=MESH,
        )
        return c

    def greet_dp(k, c):
        pl.semaphore_signal(
            barrier, inc=1, device_id={"dp": lax.rem(my_dp + k, n_dp)}, device_id_type=MESH
        )
        return c

    lax.fori_loop(1, n_context, greet, 0)
    lax.fori_loop(1, n_dp, greet_dp, 0)
    pl.semaphore_wait(barrier, n_context - 1 + n_dp - 1)

    rho = jnp.where(is_prompt, resets[0, prompt_index], TOK)

    def cols(h):
        return pl.ds(pl.multiple_of(h * HD, HD), HD)

    def column_weights(h):
        lam = rate[h]
        t = lax.broadcasted_iota(jnp.int32, (TOK, 1), 0)
        tf = t.astype(F32)
        into = jnp.where(t < rho, jnp.exp(-lam * (tf + 1.0)), 0.0)
        out = jnp.where(t >= lax.rem(rho, TOK), jnp.exp(-lam * (TOK - 1.0 - tf)), 0.0)
        return into, out

    def decay_row(h):
        return jnp.exp(jnp.full((1, HD), -float(TOK) * rate[h], F32))

    def link(h, j, row):
        return row * (resets[0, j] == TOK).astype(F32)

    def my_link(h):
        return decay_row(h) * (rho == TOK).astype(F32)

    def slice_of(ww):
        return pl.ds(pl.multiple_of(ww * SL, SL), SL)

    def part(p):
        return pl.ds(pl.multiple_of(p * PR, PR), PR)

    def owner_ctx(ww):
        return (ww // ROW) * ((ROWS - 1) * ROW) + lax.rem(ww, ROW)

    def any_wait(ref, sems, phase, h):
        return remote(ref, ref, ss.at[phase, h], sems.at[phase, h], context=owner_ctx(0))

    def stage_a(h, c):
        _, out = column_weights(h)
        kw = k_ref[:, cols(h)].astype(F32) * (out * scale)
        hi, lo = split(kw)
        vh = v_ref[:, cols(h)]
        l_buf[h] = dot(hi, vh, 0, 0) + dot(lo, vh, 0, 0)

        @pl.when(is_prompt)
        def _():
            def one(k, cc):
                ww = lax.rem(k, 2) * ROW + lax.rem(z + k // 2, ROW)
                remote(
                    l_buf.at[h, slice_of(ww)],
                    r1.at[h, prompt_index],
                    ss.at[0, h],
                    rs.at[0, h],
                    context=owner_ctx(ww),
                ).start()
                return cc

            lax.fori_loop(0, OWNERS, one, 0)

        return c

    loads[0].wait()
    loads[1].wait()
    lax.fori_loop(0, heads, stage_a, 0)

    def stage_b(h):
        any_wait(r1.at[h], rs, 0, h).wait_recv()
        row = decay_row(h)

        def per_block(b, carry):
            o2[h, b] = carry[0]

            def step(mm, inner):
                s, c0, c1 = inner
                j = b * SPAN + mm
                s = s * link(h, j, row) + r1[h, j]
                c0 = c0 + s * (pairs[0, 0] == j).astype(F32)
                c1 = c1 + s * (pairs[0, 1] == j).astype(F32)
                return s, c0, c1

            return lax.fori_loop(0, SPAN, step, carry)

        zero = jnp.zeros((SL, HD), F32)
        _, c0, c1 = lax.fori_loop(0, PROMPTS // SPAN, per_block, (zero, zero, zero))
        o2[h, 4] = c0
        o2[h, 5] = c1

        def to_prompt(b, c):
            remote(
                o2.at[h, b],
                s_buf.at[h, slice_of(w)],
                ss.at[1, h],
                rs.at[1, h],
                context=ROW + b * SPAN,
            ).start()
            return c

        lax.fori_loop(1, PROMPTS // SPAN, to_prompt, 0)

        def to_response(k, c):
            target = (k // 2) * ((ROWS - 1) * ROW) + lax.rem(k, 2) * SPAN

            @pl.when(target != me)
            def _():
                remote(
                    o2.at[h, 4 + k // 2],
                    s_buf.at[h, slice_of(w)],
                    ss.at[1, h],
                    rs.at[1, h],
                    context=target,
                ).start()

            @pl.when(target == me)
            def _():
                s_buf[h, slice_of(w), :] = o2[h, 4 + k // 2]

            return c

        lax.fori_loop(0, 4, to_response, 0)

    def chain(h):
        @pl.when(start_of_all)
        def _():
            s_buf[h] = jnp.zeros((HD, HD), F32)

        @pl.when(jnp.logical_and(first_prompt, jnp.logical_not(start_of_all)))
        def _():
            any_wait(s_buf.at[h], rs, 1, h).wait_recv()

        @pl.when(first_response)
        def _():
            any_wait(s_buf.at[h, pl.ds(0, HD - SL)], rs, 1, h).wait_recv()

        factor = my_link(h)

        def step(p, c):
            here = s_buf.at[h, part(p)]

            @pl.when(m > 0)
            def _():
                remote(here, here, cs.at[h, p], cr.at[h, p], context=me).wait_recv()

            @pl.when(m < SPAN - 1)
            def _():
                eo_buf[h, part(p), :] = s_buf[h, part(p), :] * factor + l_buf[h, part(p), :]
                remote(
                    eo_buf.at[h, part(p)], here, cs.at[h, p], cr.at[h, p], context=me + 1
                ).start()

            return c

        lax.fori_loop(0, PARTS, step, 0)

    def store(src, dst, kind, h):
        pltpu.make_async_copy(src.at[:, cols(h)], dst.at[:, cols(h)], out_sem.at[kind]).start()

    def stage_c(h):
        lam = rate[h]
        into, out = column_weights(h)
        ti = lax.broadcasted_iota(jnp.int32, (TOK, TOK), 0)
        si = lax.broadcasted_iota(jnp.int32, (TOK, TOK), 1)
        dist = (ti - si).astype(F32)
        allowed = (ti >= si) & ((ti >= rho) == (si >= rho))
        mask = jnp.where(allowed, jnp.exp(-lam * jnp.maximum(dist, 0.0)), 0.0)
        qh, kh, vh = q_ref[:, cols(h)], k_ref[:, cols(h)], v_ref[:, cols(h)]
        weights = (dot(qh, kh, 1, 1) * scale * mask).astype(BF16)
        mixed = dot(weights, vh, 1, 0)
        s_hi, s_lo = split(s_buf[h])
        mixed = mixed + into * (dot(qh, s_hi, 1, 0) + dot(qh, s_lo, 1, 0))
        centre = mixed - jnp.mean(mixed, axis=1, keepdims=True)
        r = lax.rsqrt(jnp.mean(centre * centre, axis=1, keepdims=True) + 1e-05)
        xhat = centre * r
        gain = gain_ref[:, cols(h)]
        gate = g_ref[:, cols(h)].astype(F32)
        go = do_ref[:, cols(h)].astype(F32)
        sig = 1.0 / (1.0 + jnp.exp(-gate))
        silu = gate * sig
        ret_ref[:, cols(h)] = (silu * xhat * gain).astype(BF16)
        gox = go * xhat
        dgate_ref[:, cols(h)] = (gox * gain * (sig + silu * (1.0 - sig))).astype(BF16)
        gp[pl.ds(h, 1), :] = jnp.sum(gox * silu, axis=0, keepdims=True)
        dx = go * silu * gain
        dx = dx - jnp.mean(dx, axis=1, keepdims=True) - xhat * jnp.mean(
            dx * xhat, axis=1, keepdims=True
        )
        gm = dx * r
        e_hi, e_lo = split(gm * into)
        e_buf[h] = dot(qh, e_hi, 0, 0) + dot(qh, e_lo, 0, 0)
        low, rest = split(gm)
        gw = (dot(low, vh, 1, 1) * mask).astype(BF16)
        inter = dot(low, s_hi, 1, 1) + dot(low, s_lo, 1, 1) + dot(rest, s_hi, 1, 1)
        dq_ref[:, cols(h)] = (dot(gw, kh, 1, 0) * scale + inter * into).astype(BF16)
        dkp[h] = dot(gw, qh, 0, 0) * scale
        dvp[h] = dot(weights, low, 0, 0)
        store(ret_ref, ret_hbm, 0, h)
        store(dq_ref, dq_hbm, 1, h)
        store(dgate_ref, dgate_hbm, 4, h)

    def backward(h):
        @pl.when(m == SPAN - 1)
        def _():
            n_buf[h] = jnp.zeros((HD, HD), F32)

        factor = my_link(h)
        slot = jnp.where(is_prompt, block + 1, jnp.where(block < 2, block, block - 4))

        def step(p, c):
            here = n_buf.at[h, part(p)]

            @pl.when(m < SPAN - 1)
            def _():
                remote(here, here, bs.at[h, p], br.at[h, p], context=me).wait_recv()

            no_buf[h, part(p), :] = e_buf[h, part(p), :] + n_buf[h, part(p), :] * factor

            @pl.when(m > 0)
            def _():
                remote(
                    no_buf.at[h, part(p)], here, bs.at[h, p], br.at[h, p], context=me - 1
                ).start()

            @pl.when(jnp.logical_and(m == 0, jnp.logical_not(start_of_all)))
            def _():
                def one(k, cc):
                    ww = p * (OWNERS // PARTS) + k
                    target = owner_ctx(ww)

                    @pl.when(target != me)
                    def _():
                        remote(
                            no_buf.at[h, slice_of(ww)],
                            r3.at[h, slot],
                            ss.at[2, h],
                            rs.at[2, h],
                            context=target,
                        ).start()

                    @pl.when(target == me)
                    def _():
                        r3[h, slot] = no_buf[h, slice_of(ww), :]

                    return cc

                lax.fori_loop(0, OWNERS // PARTS, one, 0)

            return c

        lax.fori_loop(0, PARTS, step, 0)

    def stage_d(h):
        @pl.when(m == 0)
        def _():
            any_wait(r3.at[h, pl.ds(0, 6)], rs, 2, h).wait_recv()

        @pl.when(m > 0)
        def _():
            any_wait(r3.at[h], rs, 2, h).wait_recv()

        row = decay_row(h)
        s0 = r3[h, 0] + r3[h, 1]
        s1 = r3[h, 2] + r3[h, 3]

        def run(b, g):
            def step(i, g):
                j = b * SPAN + SPAN - 1 - i
                g = g + s0 * (pairs[0, 0] == j).astype(F32)
                g = g + s1 * (pairs[0, 1] == j).astype(F32)
                o4[h, j] = g
                return g * link(h, j, row)

            return lax.fori_loop(0, SPAN, step, g)

        def per_block(i, g):
            b = PROMPTS // SPAN - 1 - i
            return run(b, g) + r3[h, b + 3]

        g = lax.fori_loop(0, PROMPTS // SPAN - 1, per_block, jnp.zeros((SL, HD), F32))
        run(0, g)

        def one(k, c):
            j = lax.rem(k, 2) * ROW + lax.rem(z + k // 2, ROW)
            remote(
                o4.at[h, j],
                x_buf.at[h, slice_of(w)],
                ss.at[3, h],
                rs.at[3, h],
                context=ROW + j,
            ).start()
            return c

        lax.fori_loop(0, PROMPTS, one, 0)

    gp[...] = jnp.zeros_like(gp)

    def gain_row_send():
        def one(k, c):
            remote(
                gp, gz.at[z], gs.at[0], gr.at[0], context=x * ROW + lax.rem(z + k, ROW)
            ).start()
            return c

        lax.fori_loop(1, ROW, one, 0)
        gz[z] = gp[...]

    def gain_x_send():
        ref = gz.at[pl.ds(0, ROW - 1)]
        remote(ref, ref, gs.at[0], gr.at[0], context=me).wait()
        gx_out[...] = lax.fori_loop(1, ROW, lambda i, a: a + gz[i], gz[0])

        def one(k, c):
            remote(
                gx_out, gx.at[x], gs.at[1], gr.at[1], context=lax.rem(x + k, ROWS) * ROW + z
            ).start()
            return c

        lax.fori_loop(1, ROWS, one, 0)
        gx[x] = gx_out[...]

    def gain_dp_send():
        ref = gx.at[pl.ds(0, ROWS - 1)]
        remote(ref, ref, gs.at[1], gr.at[1], context=me).wait()
        gd_out[...] = lax.fori_loop(1, ROWS, lambda i, a: a + gx[i], gx[0])

        def one(k, c):
            remote(
                gd_out, gd.at[my_dp], gs.at[2], gr.at[2], dp=lax.rem(my_dp + k, n_dp)
            ).start()
            return c

        lax.fori_loop(1, n_dp, one, 0)
        gd[my_dp] = gd_out[...]

    for load in loads[2:]:
        load.wait()

    lag = is_owner.astype(jnp.int32)

    def valid(h):
        return jnp.logical_and(h >= 0, h < heads)

    def beat(i, c):
        @pl.when(jnp.logical_and(is_owner, i < heads))
        def _():
            stage_b(i)

        hc = i - lag

        @pl.when(valid(hc))
        def _():
            chain(hc)
            stage_c(hc)

        hb = hc - (SPAN - 1) + m

        @pl.when(valid(hb))
        def _():
            backward(hb)

        hd = i - 5

        @pl.when(jnp.logical_and(is_owner, valid(hd)))
        def _():
            stage_d(hd)

        @pl.when(hc == heads)
        def _():
            gain_row_send()

        @pl.when(i == heads + 2)
        def _():
            gain_x_send()

        return c

    lax.fori_loop(0, heads + 5, beat, 0)

    def stage_e(h, c):
        @pl.when(is_prompt)
        def _():
            any_wait(x_buf.at[h], rs, 3, h).wait_recv()
            n_buf[h] = n_buf[h] + x_buf[h]

        _, out = column_weights(h)
        out = out * scale
        g_hi, g_lo = split(n_buf[h])
        kh, vh = k_ref[:, cols(h)], v_ref[:, cols(h)]
        dk_ref[:, cols(h)] = (
            dkp[h] + out * (dot(vh, g_hi, 1, 1) + dot(vh, g_lo, 1, 1))
        ).astype(BF16)
        dv_ref[:, cols(h)] = (
            dvp[h] + out * (dot(kh, g_hi, 1, 0) + dot(kh, g_lo, 1, 0))
        ).astype(BF16)
        store(dk_ref, dk_hbm, 2, h)
        store(dv_ref, dv_hbm, 3, h)

        @pl.when(h == 1)
        def _():
            gain_dp_send()

        return c

    lax.fori_loop(0, heads, stage_e, 0)

    ref = gd.at[pl.ds(0, n_dp - 1)]
    remote(ref, ref, gs.at[2], gr.at[2], context=me).wait()
    token_total = TOK * n_context * n_dp
    dgain_ref[...] = lax.fori_loop(1, n_dp, lambda i, a: a + gd[i], gd[0]) * (token_total**-0.5)

    def drain(h, c):
        @pl.when(is_prompt)
        def _():
            any_wait(l_buf.at[h], rs, 0, h).wait_send()

        @pl.when(is_owner)
        def _():
            any_wait(o4.at[h], rs, 3, h).wait_send()

        @pl.when(jnp.logical_and(is_owner, m > 0))
        def _():
            any_wait(r1.at[h, pl.ds(0, 7)], rs, 1, h).wait_send()

        @pl.when(first_response)
        def _():
            any_wait(r1.at[h, pl.ds(0, 6)], rs, 1, h).wait_send()
            any_wait(no_buf.at[h, pl.ds(0, HD - SL)], rs, 2, h).wait_send()

        @pl.when(jnp.logical_and(first_prompt, jnp.logical_not(start_of_all)))
        def _():
            any_wait(no_buf.at[h], rs, 2, h).wait_send()

        def step(p, cc):
            ref = no_buf.at[h, part(p)]

            @pl.when(m < SPAN - 1)
            def _():
                remote(ref, ref, cs.at[h, p], cr.at[h, p], context=me).wait_send()

            @pl.when(m > 0)
            def _():
                remote(ref, ref, bs.at[h, p], br.at[h, p], context=me).wait_send()

            return cc

        lax.fori_loop(0, PARTS, step, 0)
        return c

    lax.fori_loop(0, heads, drain, 0)
    for i, (src, dst) in enumerate(
        (
            (ret_ref, ret_hbm),
            (dq_ref, dq_hbm),
            (dk_ref, dk_hbm),
            (dv_ref, dv_hbm),
            (dgate_ref, dgate_hbm),
        )
    ):
        pltpu.make_async_copy(src, dst, out_sem.at[i]).wait()


def solution(mesh):
    n_dp = mesh.shape["dp"]
    assert mesh.shape["context"] == ROW * ROWS

    def per_device(
        queries,
        key_rows,
        value_rows,
        gate_rows,
        out_grad,
        decay_rate,
        norm_gain,
        reset_offsets,
        pair_prompts,
    ):
        heads = decay_rate.shape[0]
        flat = jax.ShapeDtypeStruct(queries.shape, BF16)
        vmem = pl.BlockSpec(memory_space=pltpu.VMEM)
        smem = pl.BlockSpec(memory_space=pltpu.SMEM)
        hbm = pl.BlockSpec(memory_space=pltpu.HBM)
        state = pltpu.VMEM((heads, HD, HD), F32)
        held = pltpu.VMEM(queries.shape, BF16)
        part = pltpu.VMEM((heads, TOK, HD), F32)
        small = pltpu.VMEM((8, HD), F32)
        dma = pltpu.SemaphoreType.DMA
        outs = pl.pallas_call(
            functools.partial(kernel, heads, n_dp),
            out_shape=(flat,) * 5 + (jax.ShapeDtypeStruct((8, HD), F32),),
            in_specs=[smem] * 3 + [vmem] + [hbm] * 5,
            out_specs=(hbm,) * 5 + (vmem,),
            scratch_shapes=[held] * 10
            + [state] * 7
            + [pltpu.VMEM((heads, n, SL, HD), F32) for n in (PROMPTS, 6, 7, PROMPTS)]
            + [
                part,
                part,
                small,
                pltpu.VMEM((ROW, 8, HD), F32),
                small,
                pltpu.VMEM((ROWS, 8, HD), F32),
                small,
                pltpu.VMEM((n_dp, 8, HD), F32),
                dma((4, heads)),
                dma((4, heads)),
                dma((heads, PARTS)),
                dma((heads, PARTS)),
                dma((heads, PARTS)),
                dma((heads, PARTS)),
                dma((3,)),
                dma((3,)),
                dma((5,)),
                dma((5,)),
            ],
            compiler_params=pltpu.CompilerParams(
                collective_id=0, has_side_effects=True, vmem_limit_bytes=56 << 20
            ),
        )(
            decay_rate,
            reset_offsets,
            pair_prompts,
            norm_gain.reshape(1, -1),
            queries,
            key_rows,
            value_rows,
            gate_rows,
            out_grad,
        )
        return outs[:5] + (outs[5][:heads].reshape(-1),)

    rows = P(("dp", "context"), "tensor")
    in_specs = (rows,) * 5 + (P("tensor"), P("tensor"), P("dp", None), P("dp", None))
    return jax.shard_map(
        per_device,
        mesh=mesh,
        in_specs=in_specs,
        out_specs=(rows,) * 5 + (P("tensor"),),
        check_vma=False,
    )
```

time: 136 us -> 156 us (1.15)
  Pallas kernels: 124 us -> 147 us
    pallas_call x1, Pallas kernels: 124 us -> 147 us  [per_device(): pl.pallas_call(functools.partial(kernel, heads, n_dp), out_shape=(flat,)...]
    unnamed x21 -> x15, local copies, waits for them, and re-layouts: 8.49 us -> 6.45 us
where the time goes in v2:
time: 156 us
  Pallas kernels  147 us (94%)
  local copies, waits for them, and re-layouts  8.34 us (5%)
    pallas_call x1, Pallas kernels, per_device(): pl.pallas_call(functools.partial(kernel, heads, n_dp), out_shape=(flat,)...  147 us
    unnamed x15, local copies, waits for them, and re-layouts  6.45 us

profile of v2, /device:TPU:18, one launch (start us, length us, event | category | flops | bytes accessed | tf_op | source)
XLA Modules:
  0.0 156.1 jit_solution(6339115928031358966)
XLA Ops:
  0.6 1.3 reshape.18.gain_ref
  1.9 147.1 %shard_map.136 = (bf16[128,1280]{1,0:T(8,128)(2,1)}, bf16[128,1280]{1,0:T(8,128)(2,1)}, bf16[128,1280]{1,0:T(8,128)(2,1)}, bf16[128,1280]{1,0:T(8,128)(2,1)}, bf...) custom-call(f32[5]{0:T(128)} %rate.1, s32[1,16]{1,0:T(1,128)} %resets.1, s32[1,2]{1,0:T(1,128)} %pairs.1, ...), custom_call_target="tpu_custom_call" | custom-call | tf_op jit(solution)/shard_map/pallas_call | solution.py:630
  149.0 0.0 copy-start.4
  149.1 0.7 copy-done.4
  149.7 0.6 reshape.19
  150.3 0.0 copy-start.3
  150.3 1.8 %copy.20 = bf16[128,1280]{1,0:T(8,128)(2,1)} copy(bf16[128,1280]{1,0:T(8,128)(2,1)} %get-tuple-element.24) | data formatting | bytes 655360
  152.1 0.0 copy-done.3
  152.1 0.0 copy-start.2
  152.1 0.7 copy.21
  152.8 0.4 copy-done.2
  153.2 0.0 copy-start.1
  153.2 0.7 copy.22
  153.9 0.4 copy-done.1
  154.3 0.0 copy-start
  154.3 0.7 copy.23
  155.0 0.4 copy-done
  155.4 0.7 copy.24
Async XLA Ops:
  149.0 0.7 copy-start.4
  150.3 1.8 %copy-start.3 = (bf16[128,1280]{1,0:T(8,128)(2,1)S(1)}, bf16[128,1280]{1,0:T(8,128)(2,1)}, u32[]{:S(2)}) copy-start(bf16[128,1280]{1,0:T(8,128)(2,1)} %get-tuple-element.25) | copy-start | bytes 983044
  152.1 1.1 copy-start.2
  153.2 1.1 copy-start.1
  154.3 1.1 copy-start

commit v3 on v1

--- a/solution.py
+++ b/solution.py
@@ -45,18 +45,29 @@
     rate,
     resets,
     pairs,
+    q_hbm,
+    k_hbm,
+    v_hbm,
+    g_hbm,
+    do_hbm,
+    gain_hbm,
+    ret_hbm,
+    dq_hbm,
+    dk_hbm,
+    dv_hbm,
+    dgate_hbm,
+    dgain_ref,
     q_ref,
     k_ref,
     v_ref,
     g_ref,
     do_ref,
-    gain_ref,
     ret_ref,
     dq_ref,
     dk_ref,
     dv_ref,
     dgate_ref,
-    dgain_ref,
+    gain_ref,
     l_buf,
     r1,
     o2,
@@ -85,6 +96,8 @@
     xr,
     gs,
     gr,
+    in_sem,
+    out_sem,
 ):
     me = lax.axis_index("context")
     my_dp = lax.axis_index("dp")
@@ -95,6 +108,22 @@
     def ctx(xx, zz):
         return xx * ROW + lax.rem(zz + 2 * ROW, ROW)
 
+    loads = [
+        pltpu.make_async_copy(src, dst, in_sem.at[i])
+        for i, (src, dst) in enumerate(
+            (
+                (k_hbm, k_ref),
+                (v_hbm, v_ref),
+                (q_hbm, q_ref),
+                (g_hbm, g_ref),
+                (do_hbm, do_ref),
+                (gain_hbm, gain_ref),
+            )
+        )
+    ]
+    for load in loads:
+        load.start()
+
     barrier = pltpu.get_barrier_semaphore()
 
     def greet_z(k, c):
@@ -118,8 +147,6 @@
     lax.fori_loop(1, ROW, greet_z, 0)
     lax.fori_loop(1, ROWS, greet_x, 0)
     lax.fori_loop(1, n_dp, greet_dp, 0)
-    pl.semaphore_wait(barrier, ROW - 1 + ROWS - 1 + n_dp - 1)
-
     prompt_index = jnp.clip(me - ROW, 0, 2 * ROW - 1)
     rho = jnp.where(is_prompt, resets[0, prompt_index], TOK)
 
@@ -184,10 +211,18 @@
         hi, lo = split(kw)
         vh = v_ref[:, cols(h)]
         l_buf[h] = dot(hi, vh, 0, 0) + dot(lo, vh, 0, 0)
+        return c
+
+    loads[0].wait()
+    loads[1].wait()
+    lax.fori_loop(0, heads, stage_a, 0)
+    pl.semaphore_wait(barrier, ROW - 1 + ROWS - 1 + n_dp - 1)
+
+    def send_a(h, c):
         to_owners(l_buf, r1, 0, h)
         return c
 
-    lax.fori_loop(0, heads, stage_a, 0)
+    lax.fori_loop(0, heads, send_a, 0)
 
     def decay_row(h):
         return jnp.exp(jnp.full((1, HD), -float(TOK) * rate[h], F32))
@@ -256,6 +291,21 @@
     lax.fori_loop(0, heads, stage_b, 0)
 
     gp[...] = jnp.zeros_like(gp)
+    for load in loads[2:]:
+        load.wait()
+
+    results = (
+        (ret_ref, ret_hbm),
+        (dq_ref, dq_hbm),
+        (dk_ref, dk_hbm),
+        (dv_ref, dv_hbm),
+        (dgate_ref, dgate_hbm),
+    )
+
+    def store(h, *kinds):
+        for i in kinds:
+            src, dst = results[i]
+            pltpu.make_async_copy(src.at[:, cols(h)], dst.at[:, cols(h)], out_sem.at[i]).start()
 
     def stage_c(h, c):
         lam = rate[h]
@@ -274,7 +324,7 @@
         centre = mixed - jnp.mean(mixed, axis=1, keepdims=True)
         r = lax.rsqrt(jnp.mean(centre * centre, axis=1, keepdims=True) + 1e-05)
         xhat = centre * r
-        gain = gain_ref[:, cols(h)]
+        gain = gain_ref[cols(h)].reshape(1, HD)
         gate = g_ref[:, cols(h)].astype(F32)
         go = do_ref[:, cols(h)].astype(F32)
         sig = 1.0 / (1.0 + jnp.exp(-gate))
@@ -297,6 +347,7 @@
         dq_ref[:, cols(h)] = (dot(gw, kh, 1, 0) * scale + inter * into).astype(BF16)
         dkp[h] = dot(gw, qh, 0, 0) * scale
         dvp[h] = dot(weights, low, 0, 0)
+        store(h, 0, 1, 4)
         return c
 
     lax.fori_loop(0, heads, stage_c, 0)
@@ -391,6 +442,7 @@
         dv_ref[:, cols(h)] = (
             dvp[h] + out * (dot(kh, g_hi, 1, 0) + dot(kh, g_lo, 1, 0))
         ).astype(BF16)
+        store(h, 2, 3)
 
         @pl.when(h == heads // 2)
         def _():
@@ -434,6 +486,23 @@
         return c
 
     lax.fori_loop(0, heads, drain, 0)
+    for i, (src, dst) in enumerate(results):
+        pltpu.make_async_copy(src, dst, out_sem.at[i]).wait()
+
+
+def finish_kernel(heads, *refs):
+    given, out, held, sem_in, sem_out = refs[:6], refs[6:12], refs[12:17], refs[17], refs[18]
+    loads = [pltpu.make_async_copy(given[i], held[i], sem_in.at[i]) for i in range(5)]
+    stores = [pltpu.make_async_copy(held[i], out[i], sem_out.at[i]) for i in range(5)]
+    for load in loads:
+        load.start()
+    for h in range(heads):
+        out[5][pl.ds(h * HD, HD)] = given[5][pl.ds(h, 1), :].reshape(HD)
+    for load, store in zip(loads, stores):
+        load.wait()
+        store.start()
+    for store in stores:
+        store.wait()
 
 
 def solution(mesh):
@@ -462,12 +531,17 @@
         part = pltpu.VMEM((heads, TOK, HD), F32)
         small = pltpu.VMEM((8, HD), F32)
         dma = pltpu.SemaphoreType.DMA
+        hbm = pl.BlockSpec(memory_space=pltpu.HBM)
+        anywhere = pl.BlockSpec(memory_space=pl.ANY)
+        held = pltpu.VMEM(queries.shape, BF16)
         outs = pl.pallas_call(
             functools.partial(kernel, heads, n_dp),
             out_shape=(flat, flat, flat, flat, flat, jax.ShapeDtypeStruct((8, HD), F32)),
-            in_specs=[smem] * 3 + [vmem] * 6,
-            out_specs=(vmem,) * 6,
-            scratch_shapes=[
+            in_specs=[smem] * 3 + [hbm] * 6,
+            out_specs=(hbm,) * 5 + (vmem,),
+            scratch_shapes=[held] * 10
+            + [
+                pltpu.VMEM(norm_gain.shape, F32),
                 state,
                 slots,
                 slots,
@@ -496,9 +570,11 @@
                 dma((4, heads)),
                 dma((3,)),
                 dma((3,)),
+                dma((6,)),
+                dma((5,)),
             ],
             compiler_params=pltpu.CompilerParams(
-                collective_id=0, has_side_effects=True, vmem_limit_bytes=40 << 20
+                collective_id=0, has_side_effects=True, vmem_limit_bytes=60 << 20
             ),
         )(
             decay_rate,
@@ -509,9 +585,17 @@
             value_rows,
             gate_rows,
             out_grad,
-            norm_gain.reshape(1, -1),
+            norm_gain,
         )
-        return outs[:5] + (outs[5][:heads].reshape(-1),)
+        total = jax.ShapeDtypeStruct(norm_gain.shape, F32)
+        return pl.pallas_call(
+            functools.partial(finish_kernel, heads),
+            out_shape=(flat,) * 5 + (total,),
+            in_specs=[anywhere] * 5 + [vmem],
+            out_specs=(hbm,) * 5 + (vmem,),
+            scratch_shapes=[held] * 5 + [dma((5,)), dma((5,))],
+            compiler_params=pltpu.CompilerParams(vmem_limit_bytes=60 << 20),
+        )(*outs)
 
     rows = P(("dp", "context"), "tensor")
     in_specs = (rows,) * 5 + (P("tensor"), P("tensor"), P("dp", None), P("dp", None))

time: 136 us -> 131 us (0.963)
  local copies, waits for them, and re-layouts: 9.81 us -> 0 us
  Pallas kernels: 124 us -> 130 us
    unnamed x21 -> x0, local copies, waits for them, and re-layouts: 8.49 us -> none
    pallas_call x0 -> x1, Pallas kernels: none -> 3.5 us  [per_device(): pl.pallas_call(functools.partial(finish_kernel, heads), out_shape=(flat,)...]
    pallas_call x1, Pallas kernels: 124 us -> 126 us  [per_device(): pl.pallas_call(functools.partial(kernel, heads, n_dp), out_shape=(flat, f...]
where the time goes in v3:
time: 131 us; the launch traced here: 130 us
  Pallas kernels  130 us (99%)
    pallas_call x1, Pallas kernels, per_device(): pl.pallas_call(functools.partial(kernel, heads, n_dp), out_shape=(flat, f...  126 us
    pallas_call x1, Pallas kernels, per_device(): pl.pallas_call(functools.partial(finish_kernel, heads), out_shape=(flat,)...  3.5 us

profile of v3, /device:TPU:18, one launch (start us, length us, event | category | flops | bytes accessed | tf_op | source)
XLA Modules:
  0.0 130.2 jit_solution(1555586913044185983)
XLA Ops:
  0.6 126.1 %shard_map.136 = (bf16[128,1280]{1,0:T(8,128)(2,1)}, bf16[128,1280]{1,0:T(8,128)(2,1)}, bf16[128,1280]{1,0:T(8,128)(2,1)}, bf16[128,1280]{1,0:T(8,128)(2,1)}, bf...) custom-call(f32[5]{0:T(128)} %rate.1, s32[1,16]{1,0:T(1,128)} %resets.1, s32[1,2]{1,0:T(1,128)} %pairs.1, ...), custom_call_target="tpu_custom_call" | custom-call | tf_op jit(solution)/shard_map/pallas_call | solution.py:537
  126.7 3.5 %shard_map.137 = (bf16[128,1280]{1,0:T(8,128)(2,1)}, bf16[128,1280]{1,0:T(8,128)(2,1)}, bf16[128,1280]{1,0:T(8,128)(2,1)}, bf16[128,1280]{1,0:T(8,128)(2,1)}, bf16[128,1280]{1,0:T(8,128)(2,1)}, /*index=5*/f32[1280]{0:T(1024)}) custom-call(bf16[128,1280]{1,0:T(8,128)(2,1)} %get-tuple-element.12.refs_0_, bf16[128,1280]{1,0:T(8,128)(2,1)} %get-tuple-element.13.refs_1_, ...), custom_call_target="tpu_custom_call" | custom-call | tf_op jit(solution)/shard_map/pallas_call | solution.py:591

commit v4 on v3

v4 whole, which is shorter than its diff:
```python
import functools

import jax
import jax.numpy as jnp
from jax import lax
from jax.experimental import pallas as pl
from jax.experimental.pallas import tpu as pltpu
from jax.sharding import PartitionSpec as P

MESH = pl.DeviceIdType.MESH
F32 = jnp.float32
BF16 = jnp.bfloat16

ROW = 8
ROWS = 4
HD = 256
TOK = 128
SL = HD // ROW
SPAN = 4
PARTS = 4
PR = HD // PARTS
LENT = (1, 0, 0, 0, 0)
LAG = (2, 3, 4, 5)
LAG_BACK = (6, 4, 2, 0)
LAG_SUM = 9
LAG_OWNED = 10


def dot(a, b, ca, cb):
    return lax.dot_general(a, b, (((ca,), (cb,)), ((), ())), preferred_element_type=F32)


def split(x):
    hi = x.astype(BF16)
    return hi, (x - hi.astype(F32)).astype(BF16)


def remote(src, dst, send_sem, recv_sem, **where):
    return pltpu.make_async_remote_copy(
        src_ref=src,
        dst_ref=dst,
        send_sem=send_sem,
        recv_sem=recv_sem,
        device_id=where,
        device_id_type=MESH,
    )


def pick(values, i):
    out = values[0]
    for n in range(1, len(values)):
        out = jnp.where(i == n, values[n], out)
    return out


def kernel(
    heads,
    n_dp,
    rate,
    resets,
    pairs,
    q_hbm,
    k_hbm,
    v_hbm,
    g_hbm,
    do_hbm,
    gain_hbm,
    ret_hbm,
    dq_hbm,
    dk_hbm,
    dv_hbm,
    dgate_hbm,
    dgain_ref,
    q_ref,
    k_ref,
    v_ref,
    g_ref,
    do_ref,
    ret_ref,
    dq_ref,
    dk_ref,
    dv_ref,
    dgate_ref,
    gain_ref,
    l_buf,
    s_buf,
    e_buf,
    g_buf,
    eo_buf,
    no_buf,
    r1,
    o2,
    r3,
    o4,
    t_out,
    t_in,
    seed,
    b_out,
    c_out,
    c_in,
    b_in,
    f_in,
    start,
    dkp,
    dvp,
    gp,
    gz,
    gx_out,
    gx,
    gd_out,
    gd,
    ss,
    rs,
    xs,
    xr,
    hs,
    hr,
    cs,
    cr,
    bs,
    br,
    gs,
    gr,
    in_sem,
    out_sem,
):
    me = lax.axis_index("context")
    my_dp = lax.axis_index("dp")
    x, z = me // ROW, lax.rem(me, ROW)
    m = lax.rem(z, SPAN)
    side = z // SPAN
    is_prompt = jnp.logical_and(x >= 1, x <= 2)
    is_response = jnp.logical_not(is_prompt)
    second = x >= 2
    mirror = x + 1 - 2 * lax.rem(x, 2)
    first = jnp.logical_and(is_response, m == 0)
    scale = HD**-0.5

    def ctx(xx, zz):
        return xx * ROW + lax.rem(zz + 2 * ROW, ROW)

    def lent(h):
        return pick(LENT, h) == 1

    def owns(h):
        return lent(h) == is_response

    def both(a, b):
        return jnp.logical_and(a, b)

    loads = [
        pltpu.make_async_copy(src, dst, in_sem.at[i])
        for i, (src, dst) in enumerate(
            (
                (k_hbm, k_ref),
                (v_hbm, v_ref),
                (q_hbm, q_ref),
                (g_hbm, g_ref),
                (do_hbm, do_ref),
                (gain_hbm, gain_ref),
            )
        )
    ]
    for load in loads:
        load.start()

    barrier = pltpu.get_barrier_semaphore()

    def greet(k, c):
        other = lax.rem(x + 2, ROWS) * ROW + z
        far = lax.rem(mirror + 2, ROWS) * ROW + z
        target = jnp.where(
            k < ROW,
            ctx(x, z + k),
            jnp.where(k < 2 * ROW, ctx(mirror, z + k), jnp.where(k == 2 * ROW, other, far)),
        )
        pl.semaphore_signal(barrier, inc=1, device_id={"context": target}, device_id_type=MESH)
        return c

    def greet_dp(k, c):
        pl.semaphore_signal(
            barrier, inc=1, device_id={"dp": lax.rem(my_dp + k, n_dp)}, device_id_type=MESH
        )
        return c

    lax.fori_loop(1, 2 * ROW + 2, greet, 0)
    lax.fori_loop(1, n_dp, greet_dp, 0)

    prompt_index = jnp.clip(me - ROW, 0, 2 * ROW - 1)
    rho = jnp.where(is_prompt, resets[0, prompt_index], TOK)

    def cols(h):
        return pl.ds(pl.multiple_of(h * HD, HD), HD)

    def column_weights(h):
        lam = rate[h]
        t = lax.broadcasted_iota(jnp.int32, (TOK, 1), 0)
        tf = t.astype(F32)
        into = jnp.where(t < rho, jnp.exp(-lam * (tf + 1.0)), 0.0)
        out = jnp.where(t >= lax.rem(rho, TOK), jnp.exp(-lam * (TOK - 1.0 - tf)), 0.0)
        return into, out

    def decay_row(h):
        return jnp.exp(jnp.full((1, HD), -float(TOK) * rate[h], F32))

    def link(h, j, row):
        return row * (resets[0, j] == TOK).astype(F32)

    def rows_of(zz):
        return pl.ds(pl.multiple_of(zz * SL, SL), SL)

    def part(p):
        return pl.ds(pl.multiple_of(p * PR, PR), PR)

    def spread(piece, target_row, landing, phase, h):
        def one(k, c):
            src, zz = piece(k)
            remote(
                src,
                landing(k),
                ss.at[phase, h],
                rs.at[phase, h],
                context=target_row * ROW + zz,
            ).start()
            return c

        lax.fori_loop(1, ROW, one, 0)

        @pl.when(target_row != x)
        def _():
            one(0, 0)

    def to_owners(src, dst, phase, h):
        def piece(k):
            zz = lax.rem(z + k, ROW)
            return src.at[h, rows_of(zz)], zz

        spread(piece, jnp.where(lent(h), mirror, x), lambda k: dst.at[h, k], phase, h)

        @pl.when(jnp.logical_not(lent(h)))
        def _():
            dst[h, 0] = src[h, rows_of(z)]

    def from_owner(src, dst, phase, h):
        def piece(k):
            return src.at[h, k], lax.rem(z - k + ROW, ROW)

        spread(piece, jnp.where(lent(h), mirror, x), lambda k: dst.at[h, rows_of(z)], phase, h)

        @pl.when(jnp.logical_not(lent(h)))
        def _():
            dst[h, rows_of(z)] = src[h, 0]

    def wait_slices(phase, h, sent):
        for n, when in ((ROW, lent(h)), (ROW - 1, jnp.logical_not(lent(h)))):

            @pl.when(when)
            def _():
                ref = r1.at[h, pl.ds(0, n)]
                c = remote(ref, ref, ss.at[phase, h], rs.at[phase, h], context=me)
                if sent:
                    c.wait_send()
                else:
                    c.wait_recv()

    def wait_bytes(count, send_sem, recv_sem, sent):
        ref = r1.at[0, pl.ds(0, count)]
        c = remote(ref, ref, send_sem, recv_sem, context=me)
        if sent:
            c.wait_send()
        else:
            c.wait_recv()

    def stage_a(h, c):
        _, out = column_weights(h)
        kw = k_ref[:, cols(h)].astype(F32) * (out * scale)
        hi, lo = split(kw)
        vh = v_ref[:, cols(h)]
        l_buf[h] = dot(hi, vh, 0, 0) + dot(lo, vh, 0, 0)
        return c

    loads[0].wait()
    loads[1].wait()
    lax.fori_loop(0, heads, stage_a, 0)
    pl.semaphore_wait(barrier, 2 * ROW + 1 + n_dp - 1)

    @pl.when(is_prompt)
    def _():
        def send_a(h, c):
            to_owners(l_buf, r1, 0, h)
            return c

        lax.fori_loop(0, heads, send_a, 0)

    def x_copy(src, dst, kind, h, xx):
        return remote(src, dst, xs.at[kind, h], xr.at[kind, h], context=xx * ROW + z)

    def hand_over(src, dst, kind, h, xx):
        @pl.when(xx != x)
        def _():
            x_copy(src, dst, kind, h, xx).start()

        @pl.when(xx == x)
        def _():
            dst[...] = src[...]

    def stage_b(h):
        wait_slices(0, h, False)

        @pl.when(second)
        def _():
            wait_bytes(1, xs.at[0, h], xr.at[0, h], False)
            start[...] = t_in[h]

        @pl.when(jnp.logical_not(second))
        def _():
            start[...] = jnp.zeros_like(start)

        row = decay_row(h)
        base = jnp.where(second, ROW, 0)

        def step(jz, carry):
            s, c0, c1 = carry
            j = base + jz
            slot = lax.rem(z - jz + ROW, ROW)
            o2[h, slot] = s
            s = s * link(h, j, row) + r1[h, slot]
            c0 = c0 + s * (pairs[0, 0] == j).astype(F32)
            c1 = c1 + s * (pairs[0, 1] == j).astype(F32)
            return s, c0, c1

        zero = jnp.zeros((SL, HD), F32)
        s, c0, c1 = lax.fori_loop(0, ROW, step, (start[...], zero, zero))
        c_out[h, 0] = c0
        c_out[h, 1] = c1

        @pl.when(jnp.logical_not(second))
        def _():
            t_out[h] = s
            x_copy(t_out.at[h], t_in.at[h], 0, h, jnp.where(lent(h), 3, 2)).start()

        half = second.astype(jnp.int32)
        hand_over(c_out.at[h, 0], c_in.at[h, half], 1, h, 0)
        hand_over(c_out.at[h, 1], c_in.at[h, half], 1, h, ROWS - 1)
        from_owner(o2, s_buf, 1, h)

    def wait_x(kind, h, sent):
        for n, when in ((1, lent(h)), (2, jnp.logical_not(lent(h)))):

            @pl.when(when)
            def _():
                wait_bytes(n, xs.at[kind, h], xr.at[kind, h], sent)

    def stage_seed(h):
        wait_x(1, h, False)
        seed[h] = c_in[h, 0] + c_in[h, 1]

        def one(sd, c):
            zz = sd * SPAN

            @pl.when(zz != z)
            def _():
                remote(
                    seed.at[h],
                    s_buf.at[h, rows_of(z)],
                    hs.at[0, h],
                    hr.at[0, h],
                    context=x * ROW + zz,
                ).start()

            @pl.when(zz == z)
            def _():
                s_buf[h, rows_of(z), :] = seed[h]

            return c

        lax.fori_loop(0, ROW // SPAN, one, 0)

    def chain(h):
        @pl.when(m == 0)
        def _():
            wait_bytes(ROW - 1, hs.at[0, h], hr.at[0, h], False)

        row = decay_row(h)

        def step(p, c):
            here = s_buf.at[h, part(p)]

            @pl.when(m > 0)
            def _():
                remote(here, here, cs.at[h, p], cr.at[h, p], context=me).wait_recv()

            @pl.when(m < SPAN - 1)
            def _():
                eo_buf[h, part(p), :] = s_buf[h, part(p), :] * row + l_buf[h, part(p), :]
                remote(
                    eo_buf.at[h, part(p)], here, cs.at[h, p], cr.at[h, p], context=me + 1
                ).start()

            return c

        lax.fori_loop(0, PARTS, step, 0)

    gp[...] = jnp.zeros_like(gp)
    for load in loads[2:]:
        load.wait()

    results = (
        (ret_ref, ret_hbm),
        (dq_ref, dq_hbm),
        (dk_ref, dk_hbm),
        (dv_ref, dv_hbm),
        (dgate_ref, dgate_hbm),
    )

    def store(h, *kinds):
        for i in kinds:
            src, dst = results[i]
            pltpu.make_async_copy(src.at[:, cols(h)], dst.at[:, cols(h)], out_sem.at[i]).start()

    def stage_c(h):
        lam = rate[h]
        into, out = column_weights(h)
        ti = lax.broadcasted_iota(jnp.int32, (TOK, TOK), 0)
        si = lax.broadcasted_iota(jnp.int32, (TOK, TOK), 1)
        dist = (ti - si).astype(F32)
        allowed = (ti >= si) & ((ti >= rho) == (si >= rho))
        mask = jnp.where(allowed, jnp.exp(-lam * jnp.maximum(dist, 0.0)), 0.0)
        qh, kh, vh = q_ref[:, cols(h)], k_ref[:, cols(h)], v_ref[:, cols(h)]
        weights = (dot(qh, kh, 1, 1) * scale * mask).astype(BF16)
        mixed = dot(weights, vh, 1, 0)
        s_hi, s_lo = split(s_buf[h])
        mixed = mixed + into * (dot(qh, s_hi, 1, 0) + dot(qh, s_lo, 1, 0))
        centre = mixed - jnp.mean(mixed, axis=1, keepdims=True)
        r = lax.rsqrt(jnp.mean(centre * centre, axis=1, keepdims=True) + 1e-05)
        xhat = centre * r
        gain = gain_ref[cols(h)].reshape(1, HD)
        gate = g_ref[:, cols(h)].astype(F32)
        go = do_ref[:, cols(h)].astype(F32)
        sig = 1.0 / (1.0 + jnp.exp(-gate))
        silu = gate * sig
        ret_ref[:, cols(h)] = (silu * xhat * gain).astype(BF16)
        gox = go * xhat
        dgate_ref[:, cols(h)] = (gox * gain * (sig + silu * (1.0 - sig))).astype(BF16)
        gp[pl.ds(h, 1), :] = jnp.sum(gox * silu, axis=0, keepdims=True)
        dx = go * silu * gain
        dx = dx - jnp.mean(dx, axis=1, keepdims=True) - xhat * jnp.mean(
            dx * xhat, axis=1, keepdims=True
        )
        gm = dx * r
        e_hi, e_lo = split(gm * into)
        e_buf[h] = dot(qh, e_hi, 0, 0) + dot(qh, e_lo, 0, 0)
        low, rest = split(gm)
        gw = (dot(low, vh, 1, 1) * mask).astype(BF16)
        inter = dot(low, s_hi, 1, 1) + dot(low, s_lo, 1, 1) + dot(rest, s_hi, 1, 1)
        dq_ref[:, cols(h)] = (dot(gw, kh, 1, 0) * scale + inter * into).astype(BF16)
        dkp[h] = dot(gw, qh, 0, 0) * scale
        dvp[h] = dot(weights, low, 0, 0)
        store(h, 0, 1, 4)

    def backward(h):
        @pl.when(m == SPAN - 1)
        def _():
            g_buf[h] = jnp.zeros((HD, HD), F32)

        row = decay_row(h)

        def step(p, c):
            here = g_buf.at[h, part(p)]

            @pl.when(m < SPAN - 1)
            def _():
                remote(here, here, bs.at[h, p], br.at[h, p], context=me).wait_recv()

            no_buf[h, part(p), :] = e_buf[h, part(p), :] + g_buf[h, part(p), :] * row

            @pl.when(m > 0)
            def _():
                remote(
                    no_buf.at[h, part(p)], here, bs.at[h, p], br.at[h, p], context=me - 1
                ).start()

            @pl.when(m == 0)
            def _():
                def one(k, cc):
                    zz = p * (ROW // PARTS) + k

                    @pl.when(zz != z)
                    def _():
                        remote(
                            no_buf.at[h, rows_of(zz)],
                            f_in.at[h, side],
                            hs.at[1, h],
                            hr.at[1, h],
                            context=x * ROW + zz,
                        ).start()

                    @pl.when(zz == z)
                    def _():
                        f_in[h, side] = no_buf[h, rows_of(zz), :]

                    return cc

                lax.fori_loop(0, ROW // PARTS, one, 0)

            return c

        lax.fori_loop(0, PARTS, step, 0)

    def stage_sum(h):
        @pl.when(m == 0)
        def _():
            wait_bytes(1, hs.at[1, h], hr.at[1, h], False)

        @pl.when(m > 0)
        def _():
            wait_bytes(2, hs.at[1, h], hr.at[1, h], False)

        b_out[h] = f_in[h, 0] + f_in[h, 1]
        pair = x // (ROWS - 1)
        for half in range(2):
            near = 2 - half
            target = jnp.where(lent(h), (1 - half) * (ROWS - 1), near)
            hand_over(b_out.at[h], b_in.at[h, pair], 3, h, target)

    def stage_d(h):
        wait_slices(2, h, False)
        wait_x(3, h, False)

        @pl.when(second)
        def _():
            start[...] = jnp.zeros_like(start)

        @pl.when(jnp.logical_not(second))
        def _():
            wait_bytes(1, xs.at[2, h], xr.at[2, h], False)
            start[...] = t_in[h]

        row = decay_row(h)
        base = jnp.where(second, ROW, 0)

        def step(i, g):
            jz = ROW - 1 - i
            j = base + jz
            slot = lax.rem(z - jz + ROW, ROW)
            g = g + b_in[h, 0] * (pairs[0, 0] == j).astype(F32)
            g = g + b_in[h, 1] * (pairs[0, 1] == j).astype(F32)
            o4[h, slot] = g
            return r3[h, slot] + g * link(h, j, row)

        g = lax.fori_loop(0, ROW, step, start[...])

        @pl.when(second)
        def _():
            t_out[h] = g
            x_copy(t_out.at[h], t_in.at[h], 2, h, jnp.where(lent(h), 0, 1)).start()

        from_owner(o4, g_buf, 3, h)

    def gain_row_send():
        def one(k, c):
            remote(gp, gz.at[z], gs.at[0], gr.at[0], context=ctx(x, z + k)).start()
            return c

        lax.fori_loop(1, ROW, one, 0)
        gz[z] = gp[...]

    def gain_x_send():
        ref = gz.at[pl.ds(0, ROW - 1)]
        remote(ref, ref, gs.at[0], gr.at[0], context=me).wait()
        gx_out[...] = lax.fori_loop(1, ROW, lambda i, a: a + gz[i], gz[0])

        def one(k, c):
            remote(
                gx_out, gx.at[x], gs.at[1], gr.at[1], context=lax.rem(x + k, ROWS) * ROW + z
            ).start()
            return c

        lax.fori_loop(1, ROWS, one, 0)
        gx[x] = gx_out[...]

    def gain_dp_send():
        ref = gx.at[pl.ds(0, ROWS - 1)]
        remote(ref, ref, gs.at[1], gr.at[1], context=me).wait()
        gd_out[...] = lax.fori_loop(1, ROWS, lambda i, a: a + gx[i], gx[0])

        def one(k, c):
            remote(
                gd_out, gd.at[my_dp], gs.at[2], gr.at[2], dp=lax.rem(my_dp + k, n_dp)
            ).start()
            return c

        lax.fori_loop(1, n_dp, one, 0)
        gd[my_dp] = gd_out[...]

    @pl.when(is_prompt)
    def _():
        def run_b(h, c):
            @pl.when(owns(h))
            def _():
                stage_b(h)

            return c

        lax.fori_loop(0, heads, run_b, 0)

    def valid(h):
        return both(h >= 0, h < heads)

    lag = jnp.where(is_prompt, 0, pick(LAG, m))
    lag_back = pick(LAG_BACK, m)

    def beat(i, c):
        @pl.when(is_response)
        def _():
            @pl.when(both(i < heads, owns(i)))
            def _():
                stage_b(i)

            @pl.when(valid(i - 1))
            def _():
                stage_seed(i - 1)

        hc = i - lag

        @pl.when(valid(hc))
        def _():
            @pl.when(is_prompt)
            def _():
                wait_slices(1, hc, False)

            @pl.when(is_response)
            def _():
                chain(hc)

            stage_c(hc)

            @pl.when(is_prompt)
            def _():
                to_owners(e_buf, r3, 2, hc)

        @pl.when(hc == heads)
        def _():
            gain_row_send()

        @pl.when(is_response)
        def _():
            hb = hc - lag_back

            @pl.when(valid(hb))
            def _():
                backward(hb)

            hg = i - LAG_SUM

            @pl.when(valid(hg))
            def _():
                stage_sum(hg)

        hd = i - LAG_OWNED

        @pl.when(both(valid(hd), owns(hd)))
        def _():
            stage_d(hd)

        return c

    lax.fori_loop(0, heads + LAG_OWNED, beat, 0)
    gain_x_send()

    def stage_e(h, c):
        @pl.when(is_prompt)
        def _():
            wait_slices(3, h, False)

        _, out = column_weights(h)
        out = out * scale
        g_hi, g_lo = split(g_buf[h])
        kh, vh = k_ref[:, cols(h)], v_ref[:, cols(h)]
        dk_ref[:, cols(h)] = (
            dkp[h] + out * (dot(vh, g_hi, 1, 1) + dot(vh, g_lo, 1, 1))
        ).astype(BF16)
        dv_ref[:, cols(h)] = (
            dvp[h] + out * (dot(kh, g_hi, 1, 0) + dot(kh, g_lo, 1, 0))
        ).astype(BF16)
        store(h, 2, 3)

        @pl.when(h == heads // 2)
        def _():
            gain_dp_send()

        return c

    lax.fori_loop(0, heads, stage_e, 0)

    w = gd.at[pl.ds(0, n_dp - 1)]
    remote(w, w, gs.at[2], gr.at[2], context=me).wait()
    token_total = TOK * ROW * ROWS * n_dp
    dgain_ref[...] = lax.fori_loop(1, n_dp, lambda i, a: a + gd[i], gd[0]) * (token_total**-0.5)

    def drain(h, c):
        @pl.when(is_prompt)
        def _():
            wait_slices(0, h, True)
            wait_slices(2, h, True)

        @pl.when(owns(h))
        def _():
            wait_slices(1, h, True)
            wait_slices(3, h, True)
            wait_x(1, h, True)

            @pl.when(second)
            def _():
                wait_bytes(1, xs.at[2, h], xr.at[2, h], True)

            @pl.when(jnp.logical_not(second))
            def _():
                wait_bytes(1, xs.at[0, h], xr.at[0, h], True)

        @pl.when(is_response)
        def _():
            wait_x(3, h, True)

            @pl.when(m == 0)
            def _():
                wait_bytes(1, hs.at[0, h], hr.at[0, h], True)
                wait_bytes(ROW - 1, hs.at[1, h], hr.at[1, h], True)

            @pl.when(m > 0)
            def _():
                wait_bytes(2, hs.at[0, h], hr.at[0, h], True)

            def step(p, cc):
                ref = no_buf.at[h, part(p)]

                @pl.when(m < SPAN - 1)
                def _():
                    remote(ref, ref, cs.at[h, p], cr.at[h, p], context=me).wait_send()

                @pl.when(m > 0)
                def _():
                    remote(ref, ref, bs.at[h, p], br.at[h, p], context=me).wait_send()

                return cc

            lax.fori_loop(0, PARTS, step, 0)

        return c

    lax.fori_loop(0, heads, drain, 0)
    for i, (src, dst) in enumerate(results):
        pltpu.make_async_copy(src, dst, out_sem.at[i]).wait()


def finish_kernel(heads, *refs):
    given, out, held, sem_in, sem_out = refs[:6], refs[6:12], refs[12:17], refs[17], refs[18]
    loads = [pltpu.make_async_copy(given[i], held[i], sem_in.at[i]) for i in range(5)]
    stores = [pltpu.make_async_copy(held[i], out[i], sem_out.at[i]) for i in range(5)]
    for load in loads:
        load.start()
    for h in range(heads):
        out[5][pl.ds(h * HD, HD)] = given[5][pl.ds(h, 1), :].reshape(HD)
    for load, store in zip(loads, stores):
        load.wait()
        store.start()
    for store in stores:
        store.wait()


def solution(mesh):
    n_dp = mesh.shape["dp"]
    assert mesh.shape["context"] == ROW * ROWS

    def per_device(
        queries,
        key_rows,
        value_rows,
        gate_rows,
        out_grad,
        decay_rate,
        norm_gain,
        reset_offsets,
        pair_prompts,
    ):
        heads = decay_rate.shape[0]
        flat = jax.ShapeDtypeStruct(queries.shape, BF16)
        vmem = pl.BlockSpec(memory_space=pltpu.VMEM)
        smem = pl.BlockSpec(memory_space=pltpu.SMEM)
        state = pltpu.VMEM((heads, HD, HD), F32)
        slots = pltpu.VMEM((heads, ROW, SL, HD), F32)
        piece = pltpu.VMEM((heads, SL, HD), F32)
        two = pltpu.VMEM((heads, 2, SL, HD), F32)
        part = pltpu.VMEM((heads, TOK, HD), F32)
        small = pltpu.VMEM((8, HD), F32)
        dma = pltpu.SemaphoreType.DMA
        hbm = pl.BlockSpec(memory_space=pltpu.HBM)
        anywhere = pl.BlockSpec(memory_space=pl.ANY)
        held = pltpu.VMEM(queries.shape, BF16)
        outs = pl.pallas_call(
            functools.partial(kernel, heads, n_dp),
            out_shape=(flat, flat, flat, flat, flat, jax.ShapeDtypeStruct((8, HD), F32)),
            in_specs=[smem] * 3 + [hbm] * 6,
            out_specs=(hbm,) * 5 + (vmem,),
            scratch_shapes=[held] * 10
            + [
                pltpu.VMEM(norm_gain.shape, F32),
            ]
            + [state] * 6
            + [slots] * 4
            + [piece] * 4
            + [two] * 4
            + [
                pltpu.VMEM((SL, HD), F32),
                part,
                part,
                small,
                pltpu.VMEM((ROW, 8, HD), F32),
                small,
                pltpu.VMEM((ROWS, 8, HD), F32),
                small,
                pltpu.VMEM((n_dp, 8, HD), F32),
                dma((4, heads)),
                dma((4, heads)),
                dma((4, heads)),
                dma((4, heads)),
                dma((2, heads)),
                dma((2, heads)),
                dma((heads, PARTS)),
                dma((heads, PARTS)),
                dma((heads, PARTS)),
                dma((heads, PARTS)),
                dma((3,)),
                dma((3,)),
                dma((6,)),
                dma((5,)),
            ],
            compiler_params=pltpu.CompilerParams(
                collective_id=0, has_side_effects=True, vmem_limit_bytes=60 << 20
            ),
        )(
            decay_rate,
            reset_offsets,
            pair_prompts,
            queries,
            key_rows,
            value_rows,
            gate_rows,
            out_grad,
            norm_gain,
        )
        total = jax.ShapeDtypeStruct(norm_gain.shape, F32)
        return pl.pallas_call(
            functools.partial(finish_kernel, heads),
            out_shape=(flat,) * 5 + (total,),
            in_specs=[anywhere] * 5 + [vmem],
            out_specs=(hbm,) * 5 + (vmem,),
            scratch_shapes=[held] * 5 + [dma((5,)), dma((5,))],
            compiler_params=pltpu.CompilerParams(vmem_limit_bytes=60 << 20),
        )(*outs)

    rows = P(("dp", "context"), "tensor")
    in_specs = (rows,) * 5 + (P("tensor"), P("tensor"), P("dp", None), P("dp", None))
    return jax.shard_map(
        per_device,
        mesh=mesh,
        in_specs=in_specs,
        out_specs=(rows,) * 5 + (P("tensor"),),
        check_vma=False,
    )
```

time: 131 us -> 126 us (0.962)
  Pallas kernels: 130 us -> 125 us
    pallas_call x1, Pallas kernels: 126 us -> 122 us  [per_device(): pl.pallas_call(functools.partial(kernel, heads, n_dp), out_shape=(flat, f...]
where the time goes in v4:
time: 126 us
  Pallas kernels  125 us (99%)
    pallas_call x1, Pallas kernels, per_device(): pl.pallas_call(functools.partial(kernel, heads, n_dp), out_shape=(flat, f...  122 us
    pallas_call x1, Pallas kernels, per_device(): pl.pallas_call(functools.partial(finish_kernel, heads), out_shape=(flat,)...  3.5 us

profile of v4, /device:TPU:18, one launch (start us, length us, event | category | flops | bytes accessed | tf_op | source)
XLA Modules:
  0.0 126.1 jit_solution(10545680376051064574)
XLA Ops:
  0.6 121.9 %shard_map.136 = (bf16[128,1280]{1,0:T(8,128)(2,1)}, bf16[128,1280]{1,0:T(8,128)(2,1)}, bf16[128,1280]{1,0:T(8,128)(2,1)}, bf16[128,1280]{1,0:T(8,128)(2,1)}, bf...) custom-call(f32[5]{0:T(128)} %rate.1, s32[1,16]{1,0:T(1,128)} %resets.1, s32[1,2]{1,0:T(1,128)} %pairs.1, ...), custom_call_target="tpu_custom_call" | custom-call | tf_op jit(solution)/shard_map/pallas_call | solution.py:800
  122.6 3.5 %shard_map.137 = (bf16[128,1280]{1,0:T(8,128)(2,1)}, bf16[128,1280]{1,0:T(8,128)(2,1)}, bf16[128,1280]{1,0:T(8,128)(2,1)}, bf16[128,1280]{1,0:T(8,128)(2,1)}, bf16[128,1280]{1,0:T(8,128)(2,1)}, /*index=5*/f32[1280]{0:T(1024)}) custom-call(bf16[128,1280]{1,0:T(8,128)(2,1)} %get-tuple-element.12.refs_0_, bf16[128,1280]{1,0:T(8,128)(2,1)} %get-tuple-element.13.refs_1_, ...), custom_call_target="tpu_custom_call" | custom-call | tf_op jit(solution)/shard_map/pallas_call | solution.py:853

commit v5 on v4

--- a/solution.py
+++ b/solution.py
@@ -24,6 +24,8 @@
 LAG_BACK = (6, 4, 2, 0)
 LAG_SUM = 9
 LAG_OWNED = 10
+LAG_LENT = 13
+TURN = 1
 
 
 def dot(a, b, ca, cb):
@@ -657,7 +659,7 @@
             def _():
                 stage_sum(hg)
 
-        hd = i - LAG_OWNED
+        hd = i - jnp.where(is_response, LAG_LENT, LAG_OWNED)
 
         @pl.when(both(valid(hd), owns(hd)))
         def _():
@@ -665,10 +667,11 @@
 
         return c
 
-    lax.fori_loop(0, heads + LAG_OWNED, beat, 0)
+    lax.fori_loop(0, heads + max(LAG_OWNED, LAG_LENT), beat, 0)
     gain_x_send()
 
-    def stage_e(h, c):
+    def stage_e(i, c):
+        h = jnp.where(is_prompt, lax.rem(i + TURN, heads), i)
         @pl.when(is_prompt)
         def _():
             wait_slices(3, h, False)
@@ -685,7 +688,7 @@
         ).astype(BF16)
         store(h, 2, 3)
 
-        @pl.when(h == heads // 2)
+        @pl.when(i == heads // 2)
         def _():
             gain_dp_send()
 

time: 126 us -> 123 us (0.976)
  Pallas kernels: 125 us -> 122 us
    pallas_call x1, Pallas kernels: 122 us -> 118 us  [per_device(): pl.pallas_call(functools.partial(kernel, heads, n_dp), out_shape=(flat, f...]
where the time goes in v5:
time: 123 us
  Pallas kernels  122 us (99%)
    pallas_call x1, Pallas kernels, per_device(): pl.pallas_call(functools.partial(kernel, heads, n_dp), out_shape=(flat, f...  118 us
    pallas_call x1, Pallas kernels, per_device(): pl.pallas_call(functools.partial(finish_kernel, heads), out_shape=(flat,)...  3.5 us

profile of v5, /device:TPU:18, one launch (start us, length us, event | category | flops | bytes accessed | tf_op | source)
XLA Modules:
  0.0 122.6 jit_solution(10869890727192667608)
XLA Ops:
  0.6 118.5 %shard_map.136 = (bf16[128,1280]{1,0:T(8,128)(2,1)}, bf16[128,1280]{1,0:T(8,128)(2,1)}, bf16[128,1280]{1,0:T(8,128)(2,1)}, bf16[128,1280]{1,0:T(8,128)(2,1)}, bf...) custom-call(f32[5]{0:T(128)} %rate.1, s32[1,16]{1,0:T(1,128)} %resets.1, s32[1,2]{1,0:T(1,128)} %pairs.1, ...), custom_call_target="tpu_custom_call" | custom-call | tf_op jit(solution)/shard_map/pallas_call | solution.py:803
  119.1 3.5 %shard_map.137 = (bf16[128,1280]{1,0:T(8,128)(2,1)}, bf16[128,1280]{1,0:T(8,128)(2,1)}, bf16[128,1280]{1,0:T(8,128)(2,1)}, bf16[128,1280]{1,0:T(8,128)(2,1)}, bf16[128,1280]{1,0:T(8,128)(2,1)}, /*index=5*/f32[1280]{0:T(1024)}) custom-call(bf16[128,1280]{1,0:T(8,128)(2,1)} %get-tuple-element.12.refs_0_, bf16[128,1280]{1,0:T(8,128)(2,1)} %get-tuple-element.13.refs_1_, ...), custom_call_target="tpu_custom_call" | custom-call | tf_op jit(solution)/shard_map/pallas_call | solution.py:856

commit v6 on v5

--- a/solution.py
+++ b/solution.py
@@ -58,9 +58,9 @@
 def kernel(
     heads,
     n_dp,
-    rate,
-    resets,
-    pairs,
+    rate_hbm,
+    resets_hbm,
+    pairs_hbm,
     q_hbm,
     k_hbm,
     v_hbm,
@@ -72,7 +72,7 @@
     dk_hbm,
     dv_hbm,
     dgate_hbm,
-    dgain_ref,
+    dgain_hbm,
     q_ref,
     k_ref,
     v_ref,
@@ -84,6 +84,10 @@
     dv_ref,
     dgate_ref,
     gain_ref,
+    rate,
+    resets,
+    pairs,
+    dgain_ref,
     l_buf,
     s_buf,
     e_buf,
@@ -154,6 +158,9 @@
         pltpu.make_async_copy(src, dst, in_sem.at[i])
         for i, (src, dst) in enumerate(
             (
+                (rate_hbm, rate),
+                (resets_hbm, resets),
+                (pairs_hbm, pairs),
                 (k_hbm, k_ref),
                 (v_hbm, v_ref),
                 (q_hbm, q_ref),
@@ -188,6 +195,9 @@
     lax.fori_loop(1, 2 * ROW + 2, greet, 0)
     lax.fori_loop(1, n_dp, greet_dp, 0)
 
+    for load in loads[:3]:
+        load.wait()
+
     prompt_index = jnp.clip(me - ROW, 0, 2 * ROW - 1)
     rho = jnp.where(is_prompt, resets[0, prompt_index], TOK)
 
@@ -281,8 +291,8 @@
         l_buf[h] = dot(hi, vh, 0, 0) + dot(lo, vh, 0, 0)
         return c
 
-    loads[0].wait()
-    loads[1].wait()
+    loads[3].wait()
+    loads[4].wait()
     lax.fori_loop(0, heads, stage_a, 0)
     pl.semaphore_wait(barrier, 2 * ROW + 1 + n_dp - 1)
 
@@ -404,7 +414,7 @@
         lax.fori_loop(0, PARTS, step, 0)
 
     gp[...] = jnp.zeros_like(gp)
-    for load in loads[2:]:
+    for load in loads[5:]:
         load.wait()
 
     results = (
@@ -700,6 +710,8 @@
     remote(w, w, gs.at[2], gr.at[2], context=me).wait()
     token_total = TOK * ROW * ROWS * n_dp
     dgain_ref[...] = lax.fori_loop(1, n_dp, lambda i, a: a + gd[i], gd[0]) * (token_total**-0.5)
+    last = pltpu.make_async_copy(dgain_ref, dgain_hbm, out_sem.at[5])
+    last.start()
 
     def drain(h, c):
         @pl.when(is_prompt)
@@ -754,19 +766,30 @@
     lax.fori_loop(0, heads, drain, 0)
     for i, (src, dst) in enumerate(results):
         pltpu.make_async_copy(src, dst, out_sem.at[i]).wait()
+    last.wait()
 
 
 def finish_kernel(heads, *refs):
-    given, out, held, sem_in, sem_out = refs[:6], refs[6:12], refs[12:17], refs[17], refs[18]
-    loads = [pltpu.make_async_copy(given[i], held[i], sem_in.at[i]) for i in range(5)]
+    given, out, held, total, sem_in, sem_out = (
+        refs[:6],
+        refs[6:12],
+        refs[12:18],
+        refs[18],
+        refs[19],
+        refs[20],
+    )
+    loads = [pltpu.make_async_copy(given[i], held[i], sem_in.at[i]) for i in range(6)]
     stores = [pltpu.make_async_copy(held[i], out[i], sem_out.at[i]) for i in range(5)]
+    stores.append(pltpu.make_async_copy(total, out[5], sem_out.at[5]))
     for load in loads:
         load.start()
-    for h in range(heads):
-        out[5][pl.ds(h * HD, HD)] = given[5][pl.ds(h, 1), :].reshape(HD)
-    for load, store in zip(loads, stores):
+    for load, store in zip(loads[:5], stores):
         load.wait()
         store.start()
+    loads[5].wait()
+    for h in range(heads):
+        total[pl.ds(h * HD, HD)] = held[5][pl.ds(h, 1), :].reshape(HD)
+    stores[5].start()
     for store in stores:
         store.wait()
 
@@ -788,8 +811,6 @@
     ):
         heads = decay_rate.shape[0]
         flat = jax.ShapeDtypeStruct(queries.shape, BF16)
-        vmem = pl.BlockSpec(memory_space=pltpu.VMEM)
-        smem = pl.BlockSpec(memory_space=pltpu.SMEM)
         state = pltpu.VMEM((heads, HD, HD), F32)
         slots = pltpu.VMEM((heads, ROW, SL, HD), F32)
         piece = pltpu.VMEM((heads, SL, HD), F32)
@@ -803,11 +824,15 @@
         outs = pl.pallas_call(
             functools.partial(kernel, heads, n_dp),
             out_shape=(flat, flat, flat, flat, flat, jax.ShapeDtypeStruct((8, HD), F32)),
-            in_specs=[smem] * 3 + [hbm] * 6,
-            out_specs=(hbm,) * 5 + (vmem,),
+            in_specs=[hbm] * 9,
+            out_specs=(hbm,) * 6,
             scratch_shapes=[held] * 10
             + [
                 pltpu.VMEM(norm_gain.shape, F32),
+                pltpu.SMEM(decay_rate.shape, F32),
+                pltpu.SMEM(reset_offsets.shape, jnp.int32),
+                pltpu.SMEM(pair_prompts.shape, jnp.int32),
+                small,
             ]
             + [state] * 6
             + [slots] * 4
@@ -835,8 +860,8 @@
                 dma((heads, PARTS)),
                 dma((3,)),
                 dma((3,)),
+                dma((9,)),
                 dma((6,)),
-                dma((5,)),
             ],
             compiler_params=pltpu.CompilerParams(
                 collective_id=0, has_side_effects=True, vmem_limit_bytes=60 << 20
@@ -856,9 +881,10 @@
         return pl.pallas_call(
             functools.partial(finish_kernel, heads),
             out_shape=(flat,) * 5 + (total,),
-            in_specs=[anywhere] * 5 + [vmem],
-            out_specs=(hbm,) * 5 + (vmem,),
-            scratch_shapes=[held] * 5 + [dma((5,)), dma((5,))],
+            in_specs=[anywhere] * 6,
+            out_specs=(hbm,) * 6,
+            scratch_shapes=[held] * 5
+            + [small, pltpu.VMEM(norm_gain.shape, F32), dma((6,)), dma((6,))],
             compiler_params=pltpu.CompilerParams(vmem_limit_bytes=60 << 20),
         )(*outs)
 

time: 123 us -> 121 us (0.984)
  Pallas kernels: 122 us -> 120 us
    pallas_call x1, Pallas kernels: 3.5 us -> 2.24 us  [per_device(): pl.pallas_call(functools.partial(finish_kernel, heads), out_shape=(flat,)...]
where the time goes in v6:
time: 121 us
  Pallas kernels  120 us (99%)
    pallas_call x1, Pallas kernels, per_device(): pl.pallas_call(functools.partial(kernel, heads, n_dp), out_shape=(flat, f...  118 us

profile of v6, /device:TPU:18, one launch (start us, length us, event | category | flops | bytes accessed | tf_op | source)
XLA Modules:
  0.0 120.6 jit_solution(6161568139607936253)
XLA Ops:
  0.6 117.7 %shard_map.136 = (bf16[128,1280]{1,0:T(8,128)(2,1)}, bf16[128,1280]{1,0:T(8,128)(2,1)}, bf16[128,1280]{1,0:T(8,128)(2,1)}, bf16[128,1280]{1,0:T(8,128)(2,1)}, bf...) custom-call(f32[5]{0:T(128)} %rate_hbm.1, s32[1,16]{1,0:T(1,128)} %resets_hbm.1, s32[1,2]{1,0:T(1,128)} %pairs_hbm.1, ...), custom_call_target="tpu_custom_call" | custom-call | tf_op jit(solution)/shard_map/pallas_call | solution.py:824
  118.3 2.2 %shard_map.137 = (bf16[128,1280]{1,0:T(8,128)(2,1)}, bf16[128,1280]{1,0:T(8,128)(2,1)}, bf16[128,1280]{1,0:T(8,128)(2,1)}, bf16[128,1280]{1,0:T(8,128)(2,1)}, bf16[128,1280]{1,0:T(8,128)(2,1)}, /*index=5*/f32[1280]{0:T(1024)}) custom-call(bf16[128,1280]{1,0:T(8,128)(2,1)} %get-tuple-element.12.refs_0_, bf16[128,1280]{1,0:T(8,128)(2,1)} %get-tuple-element.13.refs_1_, ...), custom_call_target="tpu_custom_call" | custom-call | tf_op jit(solution)/shard_map/pallas_call | solution.py:881

commit v7 on v6

--- a/solution.py
+++ b/solution.py
@@ -293,16 +293,21 @@
 
     loads[3].wait()
     loads[4].wait()
-    lax.fori_loop(0, heads, stage_a, 0)
+    stage_a(0, 0)
     pl.semaphore_wait(barrier, 2 * ROW + 1 + n_dp - 1)
 
-    @pl.when(is_prompt)
-    def _():
-        def send_a(h, c):
+    def send_a(h, c):
+        @pl.when(is_prompt)
+        def _():
             to_owners(l_buf, r1, 0, h)
-            return c
-
-        lax.fori_loop(0, heads, send_a, 0)
+
+        @pl.when(h + 1 < heads)
+        def _():
+            stage_a(h + 1, 0)
+
+        return c
+
+    lax.fori_loop(0, heads, send_a, 0)
 
     def x_copy(src, dst, kind, h, xx):
         return remote(src, dst, xs.at[kind, h], xr.at[kind, h], context=xx * ROW + z)

time: 121 us -> 120 us (level)
  no operation moved by 1% of the time
where the time goes in v7:
time: 120 us
  Pallas kernels  119 us (99%)
    pallas_call x1, Pallas kernels, per_device(): pl.pallas_call(functools.partial(kernel, heads, n_dp), out_shape=(flat, f...  117 us

profile of v7, /device:TPU:18, one launch (start us, length us, event | category | flops | bytes accessed | tf_op | source)
XLA Modules:
  0.0 119.8 jit_solution(101279941470892938)
XLA Ops:
  0.6 116.9 %shard_map.136 = (bf16[128,1280]{1,0:T(8,128)(2,1)}, bf16[128,1280]{1,0:T(8,128)(2,1)}, bf16[128,1280]{1,0:T(8,128)(2,1)}, bf16[128,1280]{1,0:T(8,128)(2,1)}, bf...) custom-call(f32[5]{0:T(128)} %rate_hbm.1, s32[1,16]{1,0:T(1,128)} %resets_hbm.1, s32[1,2]{1,0:T(1,128)} %pairs_hbm.1, ...), custom_call_target="tpu_custom_call" | custom-call | tf_op jit(solution)/shard_map/pallas_call | solution.py:829
  117.5 2.2 %shard_map.137 = (bf16[128,1280]{1,0:T(8,128)(2,1)}, bf16[128,1280]{1,0:T(8,128)(2,1)}, bf16[128,1280]{1,0:T(8,128)(2,1)}, bf16[128,1280]{1,0:T(8,128)(2,1)}, bf16[128,1280]{1,0:T(8,128)(2,1)}, /*index=5*/f32[1280]{0:T(1024)}) custom-call(bf16[128,1280]{1,0:T(8,128)(2,1)} %get-tuple-element.12.refs_0_, bf16[128,1280]{1,0:T(8,128)(2,1)} %get-tuple-element.13.refs_1_, ...), custom_call_target="tpu_custom_call" | custom-call | tf_op jit(solution)/shard_map/pallas_call | solution.py:886
